TPU v7x, 32 devices: a whole 2x2x4 slice. The times are simulated.
32 devices in a mesh: aux: 8 (over z, y), row: 4 (over x, core).
Axes of the slice: x: 2, y: 2, z: 4, core: 2. Of those that a mesh axis runs over, the one named last changes fastest.
Arguments:
- rho_real: float32 [128, 128, 128], P('aux', 'row'), may hold values from -6 to 6
- rho_imag: float32 [128, 128, 128], P('aux', 'row'), may hold values from -6 to 6
- hamiltonian: float32 [128, 128], replicated, may hold values from -0.5 to 0.5
- damping: float32 [128], P('aux'), may hold values from 0.2 to 2
- couplings: int32 [128, 3, 6], P('aux'), may hold values from 0 to 127, as said below
- mode_vector: float32 [128, 128], replicated, may hold values from -4 to 4
- mode_coef: float32 [2, 128], replicated, may hold values from -1 to 1
Outputs:
- next_real: float32 [128, 128, 128], P('aux', 'row')
- next_imag: float32 [128, 128, 128], P('aux', 'row')
Inputs may be any that keep to these rules, and one draw needn't show every extreme that they name: couplings[s,0,:] are target matrices below 128, couplings[s,1,:] modes below 128, couplings[s,2,:] weights 0 to 4. The couplings of the sources held by one index of aux name targets held by any one index of aux at most 12 times, and some pair reaches 12.
All inputs are finite; a program needn't handle non-finite values.
Results may differ from a plain program's by a relative error of at most 0.0018.
Values may be sent and summed in bfloat16 or wider, within the bound.
A program may use at most 64 MiB of HBM per device.

v0:
```python
import jax
import jax.numpy as jnp
from jax import lax
from jax.sharding import PartitionSpec as P

step_size = 0.1
high = lax.Precision.HIGHEST


def as_sent(x):
    return jax.tree.map(lambda a: a.astype(jnp.bfloat16) if a.dtype == jnp.float32 else a, x)


def shards(rho_real, rho_imag, hamiltonian, damping, couplings, mode_vector, mode_coef):
    energy = 0.5 * (hamiltonian + hamiltonian.T)
    width = energy.shape[0]
    local_aux, rows_dev, _ = rho_real.shape
    per_aux = couplings.shape[2]
    row_index = lax.axis_index("row")
    energy_rows = lax.dynamic_slice_in_dim(energy, row_index * rows_dev, rows_dev, 0)
    devices = lax.axis_size("aux")
    count = local_aux * per_aux
    slots = max(1, -(-count // devices))
    targets = couplings[:, 0, :].reshape(count)
    modes = couplings[:, 1, :].reshape(count)
    weights = couplings[:, 2, :].reshape(count)
    dest = targets // local_aux
    local_target = targets % local_aux
    order = jnp.arange(count)
    same_dest = (dest[:, None] == dest[None, :]) & (order[None, :] < order[:, None])
    ranked = jnp.sum(same_dest.astype(jnp.int32), axis=1)
    slot_of = dest * slots + ranked
    picker = (modes[:, None] == jnp.arange(mode_vector.shape[0])[None, :]).astype(jnp.float32)
    vectors = jnp.dot(picker, mode_vector, precision=high, preferred_element_type=jnp.float32)
    coefs = jnp.dot(picker, mode_coef.T, precision=high, preferred_element_type=jnp.float32)
    scaled = weights.astype(jnp.float32)
    plus = scaled * coefs[:, 1]
    minus = jnp.where(weights == 0, 1.0, scaled * coefs[:, 0])
    row_vec = lax.dynamic_slice_in_dim(vectors, row_index * rows_dev, rows_dev, 1)
    summed = row_vec[:, :, None] + vectors[:, None, :]
    differ = row_vec[:, :, None] - vectors[:, None, :]
    fac_real = (plus[:, None, None] * summed).reshape(local_aux, per_aux, rows_dev, width)
    fac_imag = (-(minus[:, None, None] * differ)).reshape(local_aux, per_aux, rows_dev, width)
    marks = jnp.zeros((devices * slots, local_aux), jnp.bfloat16).at[slot_of, local_target].set(1.0)
    rate = damping[:, None, None]

    def derivative(real_part, imag_part):
        zeros_block = jnp.zeros_like(real_part)
        left_real = zeros_block + jnp.einsum(
            "ij,ajk->aik",
            energy_rows,
            lax.all_gather(as_sent(real_part), "row", axis=1, tiled=True),
            precision=high,
        )
        left_imag = zeros_block + jnp.einsum(
            "ij,ajk->aik",
            energy_rows,
            lax.all_gather(as_sent(imag_part), "row", axis=1, tiled=True),
            precision=high,
        )
        prod_real = left_real - jnp.einsum("aij,jk->aik", real_part, energy, precision=high)
        prod_imag = left_imag - jnp.einsum("aij,jk->aik", imag_part, energy, precision=high)
        source_real = real_part[:, None]
        source_imag = imag_part[:, None]
        term_real = (
            (fac_real * source_real - fac_imag * source_imag)
            .astype(jnp.bfloat16)
            .reshape(count, rows_dev, width)
        )
        term_imag = (
            (fac_real * source_imag + fac_imag * source_real)
            .astype(jnp.bfloat16)
            .reshape(count, rows_dev, width)
        )
        send_real = (
            jnp.zeros((devices * slots, rows_dev, width), jnp.bfloat16).at[slot_of].set(term_real)
        )
        send_imag = (
            jnp.zeros((devices * slots, rows_dev, width), jnp.bfloat16).at[slot_of].set(term_imag)
        )
        got_real, got_imag, got_marks = (
            lax.all_to_all(send_real, "aux", split_axis=0, concat_axis=0, tiled=True),
            lax.all_to_all(send_imag, "aux", split_axis=0, concat_axis=0, tiled=True),
            lax.all_to_all(marks, "aux", split_axis=0, concat_axis=0, tiled=True),
        )
        incoming_real = jnp.einsum(
            "sa,srp->arp", got_marks, got_real, preferred_element_type=jnp.float32
        )
        incoming_imag = jnp.einsum(
            "sa,srp->arp", got_marks, got_imag, preferred_element_type=jnp.float32
        )
        out_real = prod_imag - rate * real_part + incoming_real
        out_imag = -prod_real - rate * imag_part + incoming_imag
        return (out_real, out_imag)

    state_real, state_imag = (rho_real, rho_imag)
    one_real, one_imag = derivative(state_real, state_imag)
    two_real, two_imag = derivative(
        state_real + 0.5 * step_size * one_real, state_imag + 0.5 * step_size * one_imag
    )
    three_real, three_imag = derivative(
        state_real + 0.5 * step_size * two_real, state_imag + 0.5 * step_size * two_imag
    )
    four_real, four_imag = derivative(
        state_real + step_size * three_real, state_imag + step_size * three_imag
    )
    state_real = state_real + step_size / 6.0 * (
        one_real + 2.0 * two_real + 2.0 * three_real + four_real
    )
    state_imag = state_imag + step_size / 6.0 * (
        one_imag + 2.0 * two_imag + 2.0 * three_imag + four_imag
    )
    return (state_real, state_imag)


def solution(mesh):
    placed = (
        P("aux", "row", None),
        P("aux", "row", None),
        P(),
        P("aux"),
        P("aux", None, None),
        P(),
        P(),
    )
    return jax.shard_map(
        shards,
        mesh=mesh,
        in_specs=placed,
        out_specs=(P("aux", "row", None), P("aux", "row", None)),
        check_vma=False,
    )
```

profile of v0, /device:TPU:0, one launch (start us, length us, event | category | flops | bytes accessed | tf_op | source)
XLA Modules:
  0.0 266.9 jit_solution(9758350286163717823)
XLA Ops:
  1.9 5.5 %scatter_fusion = bf16[96,16]{0,1:T(8,128)(2,1)S(1)} fusion(bf16[96,16]{0,1:T(8,128)(2,1)S(1)} %broadcast_in_dim.7, s32[96]{0:T(128)S(1)} %get-tuple-element.14, bf16[96]{0:T(256)(128)(2,1)S(1)} %broadcast.330), kind=kCustom, calls=%fused_computation | custom fusion | bytes 1344 | tf_op jit(solution)/shard_map/scatter | solution.py:44
  8.1 7.3 %all-to-all-start = ((bf16[8,12,16]{1,2,0:T(8,128)(2,1)}), bf16[8,12,16]{1,2,0:T(8,128)(2,1)S(1)}, u32[]{:S(2)}, u32[]{:S(2)}) async-start(bf16[8,12,16]{1,2,0:T(8,128)(2,1)} %copy.81), calls=%async_computation | async-start | bytes 65536 | tf_op jit(solution)/shard_map/all_to_all | solution.py:84
  19.2 10.4 %scatter_fusion.1 = bf16[96,32,128]{2,1,0:T(8,128)(2,1)} fusion(bf16[96,32,128]{2,1,0:T(8,128)(2,1)} %broadcast.308.clone.3, s32[96]{0:T(128)S(1)} %bitcast.210, bf16[96,32,128]{2,1,0:T(8,128)(2,1)S(1)} %get-tuple-element.22), kind=kCustom, calls=%fused_computation.1 | custom fusion | bytes 2359680 | tf_op jit(solution)/shard_map/scatter | solution.py:76
  29.6 6.1 %all-to-all-start.1 = ((bf16[96,32,128]{2,1,0:T(8,128)(2,1)}), bf16[96,32,128]{2,1,0:T(8,128)(2,1)S(1)}, u32[]{:S(2)}, u32[]{:S(2)}) async-start(bf16[96,32,128]{2,1,0:T(8,128)(2,1)} %scatter_fusion.1), calls=%async_computation.1 | async-start | bytes 1572864 | tf_op jit(solution)/shard_map/all_to_all | solution.py:82
  36.9 10.4 %scatter_fusion.2 = bf16[96,32,128]{2,1,0:T(8,128)(2,1)} fusion(bf16[96,32,128]{2,1,0:T(8,128)(2,1)} %broadcast.308.clone.2, s32[96]{0:T(128)S(1)} %bitcast.211, bf16[96,32,128]{2,1,0:T(8,128)(2,1)S(1)} %get-tuple-element.23), kind=kCustom, calls=%fused_computation.2 | custom fusion | bytes 2359680 | tf_op jit(solution)/shard_map/scatter | solution.py:79
  47.3 8.1 %all-to-all-done.1 = bf16[96,32,128]{2,1,0:T(8,128)(2,1)S(1)} async-done(((bf16[96,32,128]{2,1,0:T(8,128)(2,1)}), bf16[96,32,128]{2,1,0:T(8,128)(2,1)S(1)}, u32[]{:S(2)}, u32[]{:S(2)}) %all-to-all-start.1) | async-done | bytes 786464 | tf_op jit(solution)/shard_map/all_to_all | solution.py:82
  55.5 3.5 %all-to-all-start.2 = ((bf16[96,32,128]{2,1,0:T(8,128)(2,1)}), bf16[96,32,128]{2,1,0:T(8,128)(2,1)S(1)}, u32[]{:S(2)}, u32[]{:S(2)}) async-start(bf16[96,32,128]{2,1,0:T(8,128)(2,1)} %scatter_fusion.2), calls=%async_computation.2 | async-start | bytes 1572864 | tf_op jit(solution)/shard_map/all_to_all | solution.py:83
  59.0 7.2 %all_gather.24 = bf16[16,128,128]{2,1,0:T(8,128)(2,1)S(1)} all-gather(bf16[16,32,128]{2,1,0:T(8,128)(2,1)S(1)} %convert_element_type.73), channel_id=1, replica_groups=mesh['aux'=8,'row'=4] {'row'}, dimensions={1}, use_global_device_ids=true | all-gather | bytes 655360 | tf_op jit(solution)/shard_map/all_gather | solution.py:58
  69.9 7.3 %all_gather.25 = bf16[16,128,128]{2,1,0:T(8,128)(2,1)S(1)} all-gather(bf16[16,32,128]{2,1,0:T(8,128)(2,1)S(1)} %get-tuple-element.24), channel_id=1, replica_groups=mesh['aux'=8,'row'=4] {'row'}, dimensions={1}, use_global_device_ids=true | all-gather | bytes 655360 | tf_op jit(solution)/shard_map/all_gather | solution.py:52
  82.8 10.4 %scatter_fusion.3 = bf16[96,32,128]{2,1,0:T(8,128)(2,1)} fusion(bf16[96,32,128]{2,1,0:T(8,128)(2,1)} %broadcast.308.clone.4, s32[96]{0:T(128)S(1)} %bitcast.212, bf16[96,32,128]{2,1,0:T(8,128)(2,1)S(1)} %get-tuple-element.21), kind=kCustom, calls=%fused_computation.3 | custom fusion | bytes 2359680 | tf_op jit(solution)/shard_map/scatter | solution.py:76
  93.2 3.7 %all-to-all-start.3 = ((bf16[96,32,128]{2,1,0:T(8,128)(2,1)}), bf16[96,32,128]{2,1,0:T(8,128)(2,1)S(1)}, u32[]{:S(2)}, u32[]{:S(2)}) async-start(bf16[96,32,128]{2,1,0:T(8,128)(2,1)} %scatter_fusion.3), calls=%async_computation.3 | async-start | bytes 1572864 | tf_op jit(solution)/shard_map/all_to_all | solution.py:82
  97.9 10.4 %scatter_fusion.4 = bf16[96,32,128]{2,1,0:T(8,128)(2,1)} fusion(bf16[96,32,128]{2,1,0:T(8,128)(2,1)} %broadcast.308.clone.1, s32[96]{0:T(128)S(1)} %bitcast.213, bf16[96,32,128]{2,1,0:T(8,128)(2,1)S(1)} %get-tuple-element.20), kind=kCustom, calls=%fused_computation.4 | custom fusion | bytes 2359680 | tf_op jit(solution)/shard_map/scatter | solution.py:79
  108.3 9.3 %all-to-all-done.3 = bf16[96,32,128]{2,1,0:T(8,128)(2,1)S(1)} async-done(((bf16[96,32,128]{2,1,0:T(8,128)(2,1)}), bf16[96,32,128]{2,1,0:T(8,128)(2,1)S(1)}, u32[]{:S(2)}, u32[]{:S(2)}) %all-to-all-start.3) | async-done | bytes 786464 | tf_op jit(solution)/shard_map/all_to_all | solution.py:82
  117.6 3.6 %all-to-all-start.4 = ((bf16[96,32,128]{2,1,0:T(8,128)(2,1)}), bf16[96,32,128]{2,1,0:T(8,128)(2,1)S(1)}, u32[]{:S(2)}, u32[]{:S(2)}) async-start(bf16[96,32,128]{2,1,0:T(8,128)(2,1)} %scatter_fusion.4), calls=%async_computation.4 | async-start | bytes 1572864 | tf_op jit(solution)/shard_map/all_to_all | solution.py:83
  121.3 6.7 %all_gather.26 = bf16[16,128,128]{2,1,0:T(8,128)(2,1)S(1)} all-gather(bf16[16,32,128]{2,1,0:T(8,128)(2,1)S(1)} %get-tuple-element.12), channel_id=1, replica_groups=mesh['aux'=8,'row'=4] {'row'}, dimensions={1}, use_global_device_ids=true | all-gather | bytes 655360 | tf_op jit(solution)/shard_map/all_gather | solution.py:58
  127.9 7.7 %all_gather.27 = bf16[16,128,128]{2,1,0:T(8,128)(2,1)S(1)} all-gather(bf16[16,32,128]{2,1,0:T(8,128)(2,1)} %get-tuple-element.8), channel_id=1, replica_groups=mesh['aux'=8,'row'=4] {'row'}, dimensions={1}, use_global_device_ids=true | all-gather | bytes 655360 | tf_op jit(solution)/shard_map/all_gather | solution.py:52
  145.1 10.4 %scatter_fusion.5 = bf16[96,32,128]{2,1,0:T(8,128)(2,1)} fusion(bf16[96,32,128]{2,1,0:T(8,128)(2,1)} %broadcast.308.clone.6, s32[96]{0:T(128)S(1)} %bitcast.214, bf16[96,32,128]{2,1,0:T(8,128)(2,1)S(1)} %get-tuple-element.18), kind=kCustom, calls=%fused_computation.5 | custom fusion | bytes 2359680 | tf_op jit(solution)/shard_map/scatter | solution.py:76
  155.5 3.6 %all-to-all-start.5 = ((bf16[96,32,128]{2,1,0:T(8,128)(2,1)}), bf16[96,32,128]{2,1,0:T(8,128)(2,1)S(1)}, u32[]{:S(2)}, u32[]{:S(2)}) async-start(bf16[96,32,128]{2,1,0:T(8,128)(2,1)} %scatter_fusion.5), calls=%async_computation.5 | async-start | bytes 1572864 | tf_op jit(solution)/shard_map/all_to_all | solution.py:82
  160.1 10.4 %scatter_fusion.6 = bf16[96,32,128]{2,1,0:T(8,128)(2,1)} fusion(bf16[96,32,128]{2,1,0:T(8,128)(2,1)} %broadcast.308.clone, s32[96]{0:T(128)S(1)} %bitcast.215, bf16[96,32,128]{2,1,0:T(8,128)(2,1)S(1)} %get-tuple-element.19), kind=kCustom, calls=%fused_computation.6 | custom fusion | bytes 2359680 | tf_op jit(solution)/shard_map/scatter | solution.py:79
  170.5 9.1 %all-to-all-done.5 = bf16[96,32,128]{2,1,0:T(8,128)(2,1)S(1)} async-done(((bf16[96,32,128]{2,1,0:T(8,128)(2,1)}), bf16[96,32,128]{2,1,0:T(8,128)(2,1)S(1)}, u32[]{:S(2)}, u32[]{:S(2)}) %all-to-all-start.5) | async-done | bytes 786464 | tf_op jit(solution)/shard_map/all_to_all | solution.py:82
  179.5 3.6 %all-to-all-start.6 = ((bf16[96,32,128]{2,1,0:T(8,128)(2,1)}), bf16[96,32,128]{2,1,0:T(8,128)(2,1)S(1)}, u32[]{:S(2)}, u32[]{:S(2)}) async-start(bf16[96,32,128]{2,1,0:T(8,128)(2,1)} %scatter_fusion.6), calls=%async_computation.6 | async-start | bytes 1572864 | tf_op jit(solution)/shard_map/all_to_all | solution.py:83
  183.1 6.8 %all_gather.28 = bf16[16,128,128]{2,1,0:T(8,128)(2,1)S(1)} all-gather(bf16[16,32,128]{2,1,0:T(8,128)(2,1)S(1)} %get-tuple-element.4), channel_id=1, replica_groups=mesh['aux'=8,'row'=4] {'row'}, dimensions={1}, use_global_device_ids=true | all-gather | bytes 655360 | tf_op jit(solution)/shard_map/all_gather | solution.py:58
  190.0 7.3 %all_gather.29 = bf16[16,128,128]{2,1,0:T(8,128)(2,1)S(1)} all-gather(bf16[16,32,128]{2,1,0:T(8,128)(2,1)S(1)} %get-tuple-element.10), channel_id=1, replica_groups=mesh['aux'=8,'row'=4] {'row'}, dimensions={1}, use_global_device_ids=true | all-gather | bytes 655360 | tf_op jit(solution)/shard_map/all_gather | solution.py:52
  199.4 4.1 %all-to-all-done.6 = bf16[96,32,128]{2,1,0:T(8,128)(2,1)S(1)} async-done(((bf16[96,32,128]{2,1,0:T(8,128)(2,1)}), bf16[96,32,128]{2,1,0:T(8,128)(2,1)S(1)}, u32[]{:S(2)}, u32[]{:S(2)}) %all-to-all-start.6) | async-done | bytes 786464 | tf_op jit(solution)/shard_map/all_to_all | solution.py:83
  207.1 10.4 %scatter_fusion.8 = bf16[96,32,128]{2,1,0:T(8,128)(2,1)} fusion(bf16[96,32,128]{2,1,0:T(8,128)(2,1)} %broadcast.308.clone.7, s32[96]{0:T(128)S(1)} %bitcast.216, bf16[96,32,128]{2,1,0:T(8,128)(2,1)S(1)} %get-tuple-element.16), kind=kCustom, calls=%fused_computation.8 | custom fusion | bytes 2359680 | tf_op jit(solution)/shard_map/scatter | solution.py:79
  217.5 3.5 %all-to-all-start.8 = ((bf16[96,32,128]{2,1,0:T(8,128)(2,1)}), bf16[96,32,128]{2,1,0:T(8,128)(2,1)S(1)}, u32[]{:S(2)}, u32[]{:S(2)}) async-start(bf16[96,32,128]{2,1,0:T(8,128)(2,1)} %scatter_fusion.8), calls=%async_computation.8 | async-start | bytes 1572864 | tf_op jit(solution)/shard_map/all_to_all | solution.py:83
  222.0 10.4 %scatter_fusion.7 = bf16[96,32,128]{2,1,0:T(8,128)(2,1)} fusion(bf16[96,32,128]{2,1,0:T(8,128)(2,1)} %broadcast.308.clone.5, s32[96]{0:T(128)S(1)} %bitcast.217, bf16[96,32,128]{2,1,0:T(8,128)(2,1)S(1)} %get-tuple-element.17), kind=kCustom, calls=%fused_computation.7 | custom fusion | bytes 2359680 | tf_op jit(solution)/shard_map/scatter | solution.py:76
  232.4 9.0 %all-to-all-done.8 = bf16[96,32,128]{2,1,0:T(8,128)(2,1)S(1)} async-done(((bf16[96,32,128]{2,1,0:T(8,128)(2,1)}), bf16[96,32,128]{2,1,0:T(8,128)(2,1)S(1)}, u32[]{:S(2)}, u32[]{:S(2)}) %all-to-all-start.8) | async-done | bytes 786464 | tf_op jit(solution)/shard_map/all_to_all | solution.py:83
  241.4 3.5 %all-to-all-start.7 = ((bf16[96,32,128]{2,1,0:T(8,128)(2,1)}), bf16[96,32,128]{2,1,0:T(8,128)(2,1)S(1)}, u32[]{:S(2)}, u32[]{:S(2)}) async-start(bf16[96,32,128]{2,1,0:T(8,128)(2,1)} %scatter_fusion.7), calls=%async_computation.7 | async-start | bytes 1572864 | tf_op jit(solution)/shard_map/all_to_all | solution.py:82
  245.0 6.9 %all_gather.31 = bf16[16,128,128]{2,1,0:T(8,128)(2,1)S(1)} all-gather(bf16[16,32,128]{2,1,0:T(8,128)(2,1)S(1)} %get-tuple-element.2), channel_id=1, replica_groups=mesh['aux'=8,'row'=4] {'row'}, dimensions={1}, use_global_device_ids=true | all-gather | bytes 655360 | tf_op jit(solution)/shard_map/all_gather | solution.py:52
  251.8 7.5 %all_gather.30 = bf16[16,128,128]{2,1,0:T(8,128)(2,1)S(1)} all-gather(bf16[16,32,128]{2,1,0:T(8,128)(2,1)} %get-tuple-element.6), channel_id=1, replica_groups=mesh['aux'=8,'row'=4] {'row'}, dimensions={1}, use_global_device_ids=true | all-gather | bytes 655360 | tf_op jit(solution)/shard_map/all_gather | solution.py:58
  261.9 3.4 %all-to-all-done.7 = bf16[96,32,128]{2,1,0:T(8,128)(2,1)S(1)} async-done(((bf16[96,32,128]{2,1,0:T(8,128)(2,1)}), bf16[96,32,128]{2,1,0:T(8,128)(2,1)S(1)}, u32[]{:S(2)}, u32[]{:S(2)}) %all-to-all-start.7) | async-done | bytes 786464 | tf_op jit(solution)/shard_map/all_to_all | solution.py:82
  (94 shorter events, 38.4 us)
Async XLA Ops:
  0.6 15.6 %copy-start = (f32[128,128]{1,0:T(8,128)S(1)}, f32[128,128]{1,0:T(8,128)}, u32[]{:S(2)}) copy-start(f32[128,128]{1,0:T(8,128)} %param.12) | copy-start | bytes 196612
  0.6 15.9 %copy-start.13 = (f32[2,128]{1,0:T(2,128)S(1)}, f32[2,128]{1,0:T(2,128)}, u32[]{:S(2)}) copy-start(f32[2,128]{1,0:T(2,128)} %param.13) | copy-start | bytes 3076
  1.9 15.3 %copy-start.1 = (f32[16,32,128]{2,1,0:T(8,128)S(1)}, f32[16,32,128]{2,1,0:T(8,128)}, u32[]{:S(2)}) copy-start(f32[16,32,128]{2,1,0:T(8,128)} %param.8) | copy-start | bytes 786436
  1.9 15.3 %copy-start.2 = (f32[16,32,128]{2,1,0:T(8,128)S(1)}, f32[16,32,128]{2,1,0:T(8,128)}, u32[]{:S(2)}) copy-start(f32[16,32,128]{2,1,0:T(8,128)} %param.7) | copy-start | bytes 786436
  8.1 21.5 %all-to-all-start = ((bf16[8,12,16]{1,2,0:T(8,128)(2,1)}), bf16[8,12,16]{1,2,0:T(8,128)(2,1)S(1)}, u32[]{:S(2)}, u32[]{:S(2)}) async-start(bf16[8,12,16]{1,2,0:T(8,128)(2,1)} %copy.81), calls=%async_computation | async-start | bytes 65536 | tf_op jit(solution)/shard_map/all_to_all | solution.py:84
  29.6 6.2 %copy-start.11 = (f32[128,128]{1,0:T(8,128)S(1)}, f32[128,128]{1,0:T(8,128)}, u32[]{:S(2)}) copy-start(f32[128,128]{1,0:T(8,128)} %param.9) | copy-start | bytes 196612
  29.6 25.8 %all-to-all-start.1 = ((bf16[96,32,128]{2,1,0:T(8,128)(2,1)}), bf16[96,32,128]{2,1,0:T(8,128)(2,1)S(1)}, u32[]{:S(2)}, u32[]{:S(2)}) async-start(bf16[96,32,128]{2,1,0:T(8,128)(2,1)} %scatter_fusion.1), calls=%async_computation.1 | async-start | bytes 1572864 | tf_op jit(solution)/shard_map/all_to_all | solution.py:82
  55.5 23.9 %all-to-all-start.2 = ((bf16[96,32,128]{2,1,0:T(8,128)(2,1)}), bf16[96,32,128]{2,1,0:T(8,128)(2,1)S(1)}, u32[]{:S(2)}, u32[]{:S(2)}) async-start(bf16[96,32,128]{2,1,0:T(8,128)(2,1)} %scatter_fusion.2), calls=%async_computation.2 | async-start | bytes 1572864 | tf_op jit(solution)/shard_map/all_to_all | solution.py:83
  67.2 0.8 copy-start.12
  67.7 1.0 copy-start.9
  93.2 24.4 %all-to-all-start.3 = ((bf16[96,32,128]{2,1,0:T(8,128)(2,1)}), bf16[96,32,128]{2,1,0:T(8,128)(2,1)S(1)}, u32[]{:S(2)}, u32[]{:S(2)}) async-start(bf16[96,32,128]{2,1,0:T(8,128)(2,1)} %scatter_fusion.3), calls=%async_computation.3 | async-start | bytes 1572864 | tf_op jit(solution)/shard_map/all_to_all | solution.py:82
  117.6 24.0 %all-to-all-start.4 = ((bf16[96,32,128]{2,1,0:T(8,128)(2,1)}), bf16[96,32,128]{2,1,0:T(8,128)(2,1)S(1)}, u32[]{:S(2)}, u32[]{:S(2)}) async-start(bf16[96,32,128]{2,1,0:T(8,128)(2,1)} %scatter_fusion.4), calls=%async_computation.4 | async-start | bytes 1572864 | tf_op jit(solution)/shard_map/all_to_all | solution.py:83
  138.5 3.5 %copy-start.3 = (f32[16,32,128]{2,1,0:T(8,128)S(1)}, f32[16,32,128]{2,1,0:T(8,128)}, u32[]{:S(2)}) copy-start(f32[16,32,128]{2,1,0:T(8,128)} %convolution_bitcast_fusion.4) | copy-start | bytes 786436
  155.5 24.0 %all-to-all-start.5 = ((bf16[96,32,128]{2,1,0:T(8,128)(2,1)}), bf16[96,32,128]{2,1,0:T(8,128)(2,1)S(1)}, u32[]{:S(2)}, u32[]{:S(2)}) async-start(bf16[96,32,128]{2,1,0:T(8,128)(2,1)} %scatter_fusion.5), calls=%async_computation.5 | async-start | bytes 1572864 | tf_op jit(solution)/shard_map/all_to_all | solution.py:82
  179.5 24.0 %all-to-all-start.6 = ((bf16[96,32,128]{2,1,0:T(8,128)(2,1)}), bf16[96,32,128]{2,1,0:T(8,128)(2,1)S(1)}, u32[]{:S(2)}, u32[]{:S(2)}) async-start(bf16[96,32,128]{2,1,0:T(8,128)(2,1)} %scatter_fusion.6), calls=%async_computation.6 | async-start | bytes 1572864 | tf_op jit(solution)/shard_map/all_to_all | solution.py:83
  217.5 23.9 %all-to-all-start.8 = ((bf16[96,32,128]{2,1,0:T(8,128)(2,1)}), bf16[96,32,128]{2,1,0:T(8,128)(2,1)S(1)}, u32[]{:S(2)}, u32[]{:S(2)}) async-start(bf16[96,32,128]{2,1,0:T(8,128)(2,1)} %scatter_fusion.8), calls=%async_computation.8 | async-start | bytes 1572864 | tf_op jit(solution)/shard_map/all_to_all | solution.py:83
  241.4 23.9 %all-to-all-start.7 = ((bf16[96,32,128]{2,1,0:T(8,128)(2,1)}), bf16[96,32,128]{2,1,0:T(8,128)(2,1)S(1)}, u32[]{:S(2)}, u32[]{:S(2)}) async-start(bf16[96,32,128]{2,1,0:T(8,128)(2,1)} %scatter_fusion.7), calls=%async_computation.7 | async-start | bytes 1572864 | tf_op jit(solution)/shard_map/all_to_all | solution.py:82
  259.6 1.0 copy-start.4
  259.6 1.0 copy-start.6
  259.6 1.1 copy-start.8
  261.9 3.7 %copy-start.5 = (f32[16,32,128]{2,1,0:T(8,128)S(1)}, f32[16,32,128]{2,1,0:T(8,128)}, u32[]{:S(2)}) copy-start(f32[16,32,128]{2,1,0:T(8,128)} %get-tuple-element.32) | copy-start | bytes 786436
  261.9 3.7 %copy-start.7 = (f32[16,32,128]{2,1,0:T(8,128)S(1)}, f32[16,32,128]{2,1,0:T(8,128)}, u32[]{:S(2)}) copy-start(f32[16,32,128]{2,1,0:T(8,128)} %get-tuple-element.35) | copy-start | bytes 786436
  261.9 3.7 %copy-start.10 = (f32[16,32,128]{2,1,0:T(8,128)S(1)}, f32[16,32,128]{2,1,0:T(8,128)}, u32[]{:S(2)}) copy-start(f32[16,32,128]{2,1,0:T(8,128)} %get-tuple-element.30) | copy-start | bytes 786436
where the time goes:
time: 271 us; the launch traced here: 267 us
  local copies, waits for them, and re-layouts  99.7 us (37%)
  blocking collectives  57.2 us (21%)
  waiting for transfers between devices  48.4 us (18%)
  starting transfers between devices  38.6 us (14%)
  matrix products  16.6 us (6%)
  other arithmetic  5.51 us (2%)
    scatter x8, local copies, waits for them, and re-layouts, derivative(): jnp.zeros((devices * slots, rows_dev, width), jnp.bfloat16).at[slot_of]  83.2 us
    all_to_all x4, waiting for transfers between devices, derivative(): lax.all_to_all(send_real, 'aux', split_axis=0, concat_axis=0, tiled=True)  29.9 us
    all_gather x4, blocking collectives, derivative(): lax.all_gather(as_sent(real_part), 'row', axis=1, tiled=True)  29.1 us
    all_gather x4, blocking collectives, derivative(): lax.all_gather(as_sent(imag_part), 'row', axis=1, tiled=True)  28.2 us
    all_to_all x4, waiting for transfers between devices, derivative(): lax.all_to_all(send_imag, 'aux', split_axis=0, concat_axis=0, tiled=True)  18.5 us
    all_to_all x4, starting transfers between devices, derivative(): lax.all_to_all(send_real, 'aux', split_axis=0, concat_axis=0, tiled=True)  17 us
    all_to_all x4, starting transfers between devices, derivative(): lax.all_to_all(send_imag, 'aux', split_axis=0, concat_axis=0, tiled=True)  14.3 us
    another operation x8, local copies, waits for them, and re-layouts  8.03 us
  transfers between devices with their start and end apart: 9, of which 8 were waited for; matrix products, arithmetic and copies ran while one was open for 26% of the time, Pallas kernels for 0%

commit v1 on v0

--- a/solution.py
+++ b/solution.py
@@ -1,17 +1,24 @@
+import functools
+
 import jax
 import jax.numpy as jnp
 from jax import lax
+from jax.experimental import pallas as pl
+from jax.experimental.pallas import tpu as pltpu
 from jax.sharding import PartitionSpec as P
 
 step_size = 0.1
 high = lax.Precision.HIGHEST
+MESH = pl.DeviceIdType.MESH
+CHUNKS = 2
+STAGES = 4
 
 
 def as_sent(x):
     return jax.tree.map(lambda a: a.astype(jnp.bfloat16) if a.dtype == jnp.float32 else a, x)
 
 
-def shards(rho_real, rho_imag, hamiltonian, damping, couplings, mode_vector, mode_coef):
+def by_terms(rho_real, rho_imag, hamiltonian, damping, couplings, mode_vector, mode_coef):
     energy = 0.5 * (hamiltonian + hamiltonian.T)
     width = energy.shape[0]
     local_aux, rows_dev, _ = rho_real.shape
@@ -113,6 +120,299 @@
     return (state_real, state_imag)
 
 
+def kernel(
+    lines,
+    row_devs,
+    half,
+    src_ref,
+    keep_ref,
+    last_ref,
+    rate_ref,
+    real_ref,
+    imag_ref,
+    energy_ref,
+    facr_ref,
+    faci_ref,
+    outr_ref,
+    outi_ref,
+    *scratch,
+):
+    n_aux, rows_dev, width = real_ref.shape
+    rows = rows_dev // CHUNKS
+    scratch = list(scratch)
+    held = [[scratch.pop(0) for _ in range(CHUNKS)] for _ in range(STAGES)]
+    full = [scratch.pop(0) for _ in range(STAGES)]
+    give = [[scratch.pop(0) for _ in range(CHUNKS)] for _ in range(STAGES)]
+    take = [[scratch.pop(0) for _ in range(CHUNKS)] for _ in range(STAGES)]
+    run, now, total, left, right, e_left, e_right, zs, zr, rs, rr, ys, yr = scratch
+
+    aux = lax.axis_index("aux")
+    row = lax.axis_index("row")
+    line = aux // 2
+    beside = aux + 1 - 2 * lax.rem(aux, 2)
+    line_peers = [lax.rem(aux + 2 * k, 2 * lines) for k in range(1, lines)]
+    row_peers = [lax.rem(row + k, row_devs) for k in range(1, row_devs)]
+    own = pl.ds(pl.multiple_of(line * n_aux, n_aux), n_aux)
+
+    barrier = pltpu.get_barrier_semaphore()
+    peers = [(p, row) for p in line_peers + [beside]] + [(aux, p) for p in row_peers]
+    for p in peers:
+        pl.semaphore_signal(barrier, inc=1, device_id=p, device_id_type=MESH)
+    pl.semaphore_wait(barrier, len(peers))
+
+    copies = []
+
+    def send(src, dst, s_sem, r_sem, device):
+        c = pltpu.make_async_remote_copy(
+            src_ref=src,
+            dst_ref=dst,
+            send_sem=s_sem,
+            recv_sem=r_sem,
+            device_id=device,
+            device_id_type=MESH,
+        )
+        c.start()
+        copies.append(c)
+        return c
+
+    line_copies, row_copies = {}, {}
+
+    def own_rows(c):
+        return pl.ds(pl.multiple_of(row * rows_dev + c * rows, rows), rows)
+
+    def share(st, c):
+        block = held[st][c].at[own]
+        line_copies[st, c] = [
+            send(block, block, zs.at[st, c, k], zr.at[st, c, k], (p, row))
+            for k, p in enumerate(line_peers)
+        ]
+        row_copies[st, c] = [
+            send(
+                block,
+                full[st].at[:, :, own_rows(c), :],
+                rs.at[st, c, k],
+                rr.at[st, c, k],
+                (aux, p),
+            )
+            for k, p in enumerate(row_peers)
+        ]
+
+    def place(st, c, a, part, x):
+        b = x.astype(jnp.bfloat16)
+        held[st][c][line * n_aux + a, part] = b
+        full[st][a, part, own_rows(c), :] = b
+
+    for c in range(CHUNKS):
+
+        @pl.loop(0, n_aux)
+        def _(a, c=c):
+            for part, ref in enumerate((real_ref, imag_ref)):
+                place(0, c, a, part, ref[a, c * rows : (c + 1) * rows, :])
+
+        share(0, c)
+
+    energy = energy_ref[...]
+    e_hi = energy.astype(jnp.bfloat16)
+    e_right[:, :width] = e_hi
+    e_right[:, width:] = (energy - e_hi.astype(jnp.float32)).astype(jnp.bfloat16)
+    mine = energy_ref[pl.ds(pl.multiple_of(row * rows_dev, rows_dev), rows_dev), :]
+    m_hi = mine.astype(jnp.bfloat16)
+    e_left[:rows_dev] = m_hi
+    e_left[rows_dev:] = (mine - m_hi.astype(jnp.float32)).astype(jnp.bfloat16)
+    run[0] = jnp.zeros(run.shape[1:], jnp.float32)
+
+    def gather_sum(st, c, group):
+        cut = slice(c * rows, (c + 1) * rows)
+
+        def body(e, acc):
+            ar, ai = acc
+            i = group * half + e
+            s = src_ref[i]
+            keep = keep_ref[i]
+            xr = held[st][c][s, 0].astype(jnp.float32)
+            xi = held[st][c][s, 1].astype(jnp.float32)
+            fr = facr_ref[i, cut, :]
+            fi = faci_ref[i, cut, :]
+            ar = keep * ar + (fr * xr - fi * xi)
+            ai = keep * ai + (fr * xi + fi * xr)
+            run[e + 1, 0] = ar
+            run[e + 1, 1] = ai
+            return ar, ai
+
+        zero = jnp.zeros((rows, width), jnp.float32)
+        lax.fori_loop(0, half, body, (zero, zero), unroll=4)
+
+    for st in range(STAGES):
+        for c in range(CHUNKS):
+            cut = slice(c * rows, (c + 1) * rows)
+            if c == 0:
+                for cc in range(CHUNKS):
+                    for d in row_copies[st, cc]:
+                        d.wait_recv()
+
+                @pl.loop(0, n_aux)
+                def _(a, st=st):
+                    for part in range(2):
+                        both = jnp.dot(
+                            e_left[...], full[st][a, part], preferred_element_type=jnp.float32
+                        )
+                        left[a, part] = both[:rows_dev] + both[rows_dev:]
+
+            flat = held[st][c][own].reshape(n_aux * 2 * rows, width)
+            both = jnp.dot(flat, e_right[...], preferred_element_type=jnp.float32)
+            right[...] = (both[:, :width] + both[:, width:]).reshape(n_aux, 2, rows, width)
+
+            for d in line_copies[st, c]:
+                d.wait_recv()
+            gather_sum(st, c, 0)
+
+            @pl.loop(0, n_aux)
+            def _(a, st=st, c=c):
+                give[st][c][a] = run[last_ref[a]].astype(jnp.bfloat16)
+
+            across = send(give[st][c], take[st][c], ys.at[st, c], yr.at[st, c], (beside, row))
+            gather_sum(st, c, 1)
+            across.wait_recv()
+
+            weight = step_size / 6.0 * (1.0 if st in (0, STAGES - 1) else 2.0)
+            ahead = step_size if st == STAGES - 2 else 0.5 * step_size
+
+            @pl.loop(0, n_aux)
+            def _(a, st=st, c=c, cut=cut, weight=weight, ahead=ahead):
+                came = run[last_ref[n_aux + a]] + take[st][c][a].astype(jnp.float32)
+                prod_r = left[a, 0, cut, :] - right[a, 0]
+                prod_i = left[a, 1, cut, :] - right[a, 1]
+                rate = rate_ref[a]
+                base_r = real_ref[a, cut, :]
+                base_i = imag_ref[a, cut, :]
+                now_r = base_r if st == 0 else now[a, 0, cut, :]
+                now_i = base_i if st == 0 else now[a, 1, cut, :]
+                k_r = prod_i - rate * now_r + came[0]
+                k_i = came[1] - prod_r - rate * now_i
+                tot_r = (base_r if st == 0 else total[a, 0, cut, :]) + weight * k_r
+                tot_i = (base_i if st == 0 else total[a, 1, cut, :]) + weight * k_i
+                if st == STAGES - 1:
+                    outr_ref[a, cut, :] = tot_r
+                    outi_ref[a, cut, :] = tot_i
+                else:
+                    total[a, 0, cut, :] = tot_r
+                    total[a, 1, cut, :] = tot_i
+                    next_r = base_r + ahead * k_r
+                    next_i = base_i + ahead * k_i
+                    now[a, 0, cut, :] = next_r
+                    now[a, 1, cut, :] = next_i
+                    place(st + 1, c, a, 0, next_r)
+                    place(st + 1, c, a, 1, next_i)
+
+            if st < STAGES - 1:
+                share(st + 1, c)
+
+    for d in copies:
+        d.wait_send()
+
+
+def by_states(rho_real, rho_imag, hamiltonian, damping, couplings, mode_vector, mode_coef):
+    energy = 0.5 * (hamiltonian + hamiltonian.T)
+    n_aux, rows_dev, width = rho_real.shape
+    per_aux = couplings.shape[2]
+    devices = lax.axis_size("aux")
+    row_devs = lax.axis_size("row")
+    lines = devices // 2
+    slots = max(1, -(-n_aux * per_aux // devices))
+    half = lines * slots
+    aux = lax.axis_index("aux")
+    row = lax.axis_index("row")
+    line, side = aux // 2, aux % 2
+
+    every = lax.all_gather(couplings, "aux", axis=0, tiled=True)
+    every = every.reshape(lines, 2, n_aux, 3, per_aux)
+    every = lax.dynamic_index_in_dim(every, side, 1, keepdims=False)
+    count = lines * n_aux * per_aux
+    targets = every[:, :, 0, :].reshape(count)
+    modes = every[:, :, 1, :].reshape(count)
+    weights = every[:, :, 2, :].reshape(count)
+    order = jnp.arange(count)
+    sources = order // per_aux
+    dest = targets // n_aux
+    chosen = dest // 2 == line
+    group = (dest % 2 == side).astype(jnp.int32)
+    key = jnp.where(chosen, group * n_aux + targets % n_aux, 2 * n_aux)
+    before = (key[None, :] < key[:, None]) | (
+        (key[None, :] == key[:, None]) & (order[None, :] < order[:, None])
+    )
+    same_group = chosen[None, :] & (group[None, :] == group[:, None])
+    ranked = jnp.sum((before & same_group).astype(jnp.int32), axis=1)
+    slot_of = jnp.where(chosen, group * half + ranked, -1)
+    pick = slot_of[None, :] == jnp.arange(2 * half)[:, None]
+
+    def picked(values):
+        return jnp.sum(jnp.where(pick, values[None, :], 0), axis=1)
+
+    src = picked(sources)
+    mode = picked(modes)
+    weight = picked(weights)
+    filled = picked(jnp.ones_like(order))
+    at_key = picked(key) + (1 - filled) * (2 * n_aux)
+    previous = jnp.concatenate([jnp.full((1,), -1, at_key.dtype), at_key[:-1]])
+    first = jnp.arange(2 * half) % half == 0
+    keep = ((at_key == previous) & ~first).astype(jnp.float32)
+    wanted = jnp.arange(2 * n_aux)
+    in_group = chosen[None, :] & (group[None, :] == wanted[:, None] // n_aux)
+    upto = jnp.sum((in_group & (key[None, :] <= wanted[:, None])).astype(jnp.int32), axis=1)
+    any_here = jnp.any(key[None, :] == wanted[:, None], axis=1)
+    last = jnp.where(any_here, upto, 0)
+
+    picker = (mode[:, None] == jnp.arange(mode_vector.shape[0])[None, :]).astype(jnp.float32)
+    vectors = jnp.dot(picker, mode_vector, precision=high, preferred_element_type=jnp.float32)
+    coefs = jnp.dot(picker, mode_coef.T, precision=high, preferred_element_type=jnp.float32)
+    scaled = weight.astype(jnp.float32)
+    there = filled.astype(jnp.float32)
+    plus = there * scaled * coefs[:, 1]
+    minus = there * jnp.where(weight == 0, 1.0, scaled * coefs[:, 0])
+    row_vec = lax.dynamic_slice_in_dim(vectors, row * rows_dev, rows_dev, 1)
+    fac_real = plus[:, None, None] * (row_vec[:, :, None] + vectors[:, None, :])
+    fac_imag = -minus[:, None, None] * (row_vec[:, :, None] - vectors[:, None, :])
+
+    rows = rows_dev // CHUNKS
+    smem = pl.BlockSpec(memory_space=pltpu.SMEM)
+    vmem = pl.BlockSpec(memory_space=pltpu.VMEM)
+    bf16, f32 = jnp.bfloat16, jnp.float32
+    piece = pltpu.VMEM((n_aux, 2, rows, width), bf16)
+    dma = pltpu.SemaphoreType.DMA
+    grid = (STAGES, CHUNKS)
+    scratch = (
+        [pltpu.VMEM((lines * n_aux, 2, rows, width), bf16)] * (STAGES * CHUNKS)
+        + [pltpu.VMEM((n_aux, 2, row_devs * rows_dev, width), bf16)] * STAGES
+        + [piece] * (2 * STAGES * CHUNKS)
+        + [
+            pltpu.VMEM((half + 1, 2, rows, width), f32),
+            pltpu.VMEM((n_aux, 2, rows_dev, width), f32),
+            pltpu.VMEM((n_aux, 2, rows_dev, width), f32),
+            pltpu.VMEM((n_aux, 2, rows_dev, width), f32),
+            pltpu.VMEM((n_aux, 2, rows, width), f32),
+            pltpu.VMEM((2 * rows_dev, width), bf16),
+            pltpu.VMEM((width, 2 * width), bf16),
+            dma(grid + (lines - 1,)),
+            dma(grid + (lines - 1,)),
+            dma(grid + (row_devs - 1,)),
+            dma(grid + (row_devs - 1,)),
+            dma(grid),
+            dma(grid),
+        ]
+    )
+    shape = jax.ShapeDtypeStruct((n_aux, rows_dev, width), f32)
+    return pl.pallas_call(
+        functools.partial(kernel, lines, row_devs, half),
+        out_shape=(shape, shape),
+        in_specs=[smem] * 4 + [vmem] * 5,
+        out_specs=(vmem, vmem),
+        scratch_shapes=scratch,
+        compiler_params=pltpu.CompilerParams(
+            collective_id=0, has_side_effects=True, vmem_limit_bytes=40 * 1024 * 1024
+        ),
+    )(src, keep, last, damping, rho_real, rho_imag, energy, fac_real, fac_imag)
+
+
 def solution(mesh):
     placed = (
         P("aux", "row", None),
@@ -123,6 +423,19 @@
         P(),
         P(),
     )
+
+    def shards(rho_real, rho_imag, hamiltonian, damping, couplings, mode_vector, mode_coef):
+        args = (rho_real, rho_imag, hamiltonian, damping, couplings, mode_vector, mode_coef)
+        devices = mesh.shape["aux"]
+        n_aux, rows_dev, _ = rho_real.shape
+        slots = max(1, -(-n_aux * couplings.shape[2] // devices))
+        terms_sent = (devices - 1) * slots
+        states_sent = devices // 2 * n_aux
+        even = devices % 2 == 0 and devices > 2 and mesh.shape["row"] > 1
+        if even and states_sent < terms_sent and rows_dev % (16 * CHUNKS) == 0:
+            return by_states(*args)
+        return by_terms(*args)
+
     return jax.shard_map(
         shards,
         mesh=mesh,

time: 271 us -> 153 us (0.56)
  the two profiles are of different devices: /device:TPU:0 before, /device:TPU:25 now
where the time goes in v1:
time: 153 us; the launch traced here: 152 us
  Pallas kernels  123 us (80%)
  blocking collectives  22.1 us (14%)
  local copies, waits for them, and re-layouts  3.94 us (3%)
  other arithmetic  2.63 us (2%)
    pallas_call x1, Pallas kernels, by_states(): pl.pallas_call(functools.partial(kernel, lines, row_devs, half), out_shap...  123 us
    all_gather x1, blocking collectives, by_states(): every = lax.all_gather(couplings, 'aux', axis=0, tiled=True)  22.1 us
    unnamed x14, local copies, waits for them, and re-layouts  3.41 us

profile of v1, /device:TPU:25, one launch (start us, length us, event | category | flops | bytes accessed | tf_op | source)
XLA Modules:
  0.0 152.5 jit_solution(14916781774574758485)
XLA Ops:
  0.6 0.0 copy-start
  0.6 0.0 copy-start.4
  0.7 0.8 copy.15
  1.5 0.9 copy.17
  2.4 0.9 fusion.3.energy_ref
  3.3 22.1 %all_gather.3 = s32[128,3,6]{2,1,0:T(4,128)S(1)} all-gather(s32[16,3,6]{2,1,0:T(4,128)S(1)} %copy.15), channel_id=1, replica_groups=mesh['aux'=8,'row'=4] {'aux'}, dimensions={0}, use_global_device_ids=true | all-gather | bytes 10368 | tf_op jit(solution)/shard_map/all_gather | solution.py:327
  25.4 0.1 broadcast_in_dim.86
  25.5 0.1 broadcast_in_dim.84
  25.7 0.1 reshape_squeeze.3
  25.9 0.1 fusion.6
  26.0 0.2 convert_reduce_fusion.1
  26.2 0.4 convert_reduce_fusion
  26.5 0.2 select_reduce_fusion.1
  26.8 0.1 and_convert_fusion.keep_ref
  26.8 0.0 copy-done.4
  26.8 0.2 fusion.5
  27.1 0.0 copy-done
  27.1 0.2 fusion.4
  27.3 0.1 constant_dynamic-slice_fusion
  27.4 0.0 copy-start.1
  27.4 0.0 copy-start.2
  27.4 0.0 copy-start.3
  27.4 0.8 subtract_multiply_fusion
  28.2 0.2 copy-done.1
  28.4 0.1 copy-done.2
  28.4 0.0 copy-done.3
  28.4 122.6 %shard_map.86 = (f32[16,32,128]{2,1,0:T(8,128)S(1)}, f32[16,32,128]{2,1,0:T(8,128)S(1)}) custom-call(s32[96]{0:T(128)S(1)} %get-tuple-element.6.src_ref, f32[96]{0:T(128)S(1)} %and_convert_fusion.keep_ref, s32[32]{0:T(128)S(1)} %broadcast_select_fusion.last_ref, f32[16]{0:T(128)S(1)} %copy-done.3, f32[16,32,128]{2,1,0:T(8,128)S(1)} %copy-done.1, ...), custom_call_target="tpu_custom_call" | custom-call | tf_op jit(solution)/shard_map/pallas_call | solution.py:404
  151.0 0.7 copy.22
  151.8 0.7 copy.23
  (10 shorter events, 0.1 us)
Async XLA Ops:
  0.6 26.5 %copy-start = (f32[128,128]{1,0:T(8,128)S(1)}, f32[128,128]{1,0:T(8,128)}, u32[]{:S(2)}) copy-start(f32[128,128]{1,0:T(8,128)} %param.12) | copy-start | bytes 196612
  0.6 26.2 %copy-start.4 = (f32[2,128]{1,0:T(2,128)S(1)}, f32[2,128]{1,0:T(2,128)}, u32[]{:S(2)}) copy-start(f32[2,128]{1,0:T(2,128)} %param.13) | copy-start | bytes 3076
  27.4 1.0 copy-start.1
  27.4 1.0 copy-start.2
  27.4 1.0 copy-start.3

commit v2 on v1

--- a/solution.py
+++ b/solution.py
@@ -120,6 +120,34 @@
     return (state_real, state_imag)
 
 
+def swap_kernel(lines, mine_ref, all_ref, local_sem, send_sem, recv_sem):
+    aux = lax.axis_index("aux")
+    row = lax.axis_index("row")
+    line = aux // 2
+    peers = [(lax.rem(aux + 2 * k, 2 * lines), row) for k in range(1, lines)]
+    keep = pltpu.make_async_copy(mine_ref, all_ref.at[line], local_sem)
+    keep.start()
+    barrier = pltpu.get_barrier_semaphore()
+    for p in peers:
+        pl.semaphore_signal(barrier, inc=1, device_id=p, device_id_type=MESH)
+    pl.semaphore_wait(barrier, len(peers))
+    copies = []
+    for k, p in enumerate(peers):
+        c = pltpu.make_async_remote_copy(
+            src_ref=mine_ref,
+            dst_ref=all_ref.at[line],
+            send_sem=send_sem.at[k],
+            recv_sem=recv_sem.at[k],
+            device_id=p,
+            device_id_type=MESH,
+        )
+        c.start()
+        copies.append(c)
+    keep.wait()
+    for c in copies:
+        c.wait()
+
+
 def kernel(
     lines,
     row_devs,
@@ -128,37 +156,53 @@
     keep_ref,
     last_ref,
     rate_ref,
-    real_ref,
-    imag_ref,
-    energy_ref,
+    real_in,
+    imag_in,
+    ham_ref,
     facr_ref,
     faci_ref,
     outr_ref,
     outi_ref,
     *scratch,
 ):
-    n_aux, rows_dev, width = real_ref.shape
+    n_aux, rows_dev, width = outr_ref.shape
     rows = rows_dev // CHUNKS
     scratch = list(scratch)
     held = [[scratch.pop(0) for _ in range(CHUNKS)] for _ in range(STAGES)]
     full = [scratch.pop(0) for _ in range(STAGES)]
     give = [[scratch.pop(0) for _ in range(CHUNKS)] for _ in range(STAGES)]
     take = [[scratch.pop(0) for _ in range(CHUNKS)] for _ in range(STAGES)]
-    run, now, total, left, right, e_left, e_right, zs, zr, rs, rr, ys, yr = scratch
+    real_ref, imag_ref, energy_ref = scratch[:3]
+    run, now, total, left, right, e_left, e_right, zs, zr, rs, rr, ys, yr, ins = scratch[3:]
+
+    fetched = [
+        pltpu.make_async_copy(real_in, real_ref, ins.at[0]),
+        pltpu.make_async_copy(imag_in, imag_ref, ins.at[1]),
+    ]
+    for f in fetched:
+        f.start()
 
     aux = lax.axis_index("aux")
     row = lax.axis_index("row")
     line = aux // 2
     beside = aux + 1 - 2 * lax.rem(aux, 2)
-    line_peers = [lax.rem(aux + 2 * k, 2 * lines) for k in range(1, lines)]
     row_peers = [lax.rem(row + k, row_devs) for k in range(1, row_devs)]
-    own = pl.ds(pl.multiple_of(line * n_aux, n_aux), n_aux)
+    last_line = lines - 1
 
     barrier = pltpu.get_barrier_semaphore()
-    peers = [(p, row) for p in line_peers + [beside]] + [(aux, p) for p in row_peers]
-    for p in peers:
+
+    @pl.when(line < last_line)
+    def _():
+        pl.semaphore_signal(barrier, inc=1, device_id=(aux + 2, row), device_id_type=MESH)
+
+    @pl.when(line > 0)
+    def _():
+        pl.semaphore_signal(barrier, inc=1, device_id=(aux - 2, row), device_id_type=MESH)
+
+    for p in [(beside, row)] + [(aux, p) for p in row_peers]:
         pl.semaphore_signal(barrier, inc=1, device_id=p, device_id_type=MESH)
-    pl.semaphore_wait(barrier, len(peers))
+    ends = (line == 0).astype(jnp.int32) + (line == last_line).astype(jnp.int32)
+    pl.semaphore_wait(barrier, 2 + row_devs - ends)
 
     copies = []
 
@@ -175,17 +219,57 @@
         copies.append(c)
         return c
 
-    line_copies, row_copies = {}, {}
+    row_copies = {}
 
     def own_rows(c):
         return pl.ds(pl.multiple_of(row * rows_dev + c * rows, rows), rows)
 
+    def block_at(st, c, at):
+        return held[st][c].at[pl.ds(pl.multiple_of(at * n_aux, n_aux), n_aux)]
+
+    def hop_copy(st, c, hop, way, at):
+        block = block_at(st, c, at)
+        return pltpu.make_async_remote_copy(
+            src_ref=block,
+            dst_ref=block,
+            send_sem=zs.at[st, c, way, hop - 1],
+            recv_sem=zr.at[st, c, way, hop - 1],
+            device_id=(aux + 2 if way == 0 else aux - 2, row),
+            device_id_type=MESH,
+        )
+
+    def hop_sends(hop, way):
+        if way == 0:
+            return (line >= hop - 1) & (line < last_line)
+        return (line + hop - 1 <= last_line) & (line > 0)
+
+    def hop_gets(hop, way):
+        return line >= hop if way == 0 else line + hop <= last_line
+
+    def hop_send(st, c, hop):
+        for way in range(2):
+
+            @pl.when(hop_sends(hop, way))
+            def _(way=way):
+                at = line - (hop - 1) if way == 0 else line + (hop - 1)
+                hop_copy(st, c, hop, way, at).start()
+
+    def hop_get(st, c, hop):
+        for way in range(2):
+
+            @pl.when(hop_gets(hop, way))
+            def _(way=way):
+                at = line - hop if way == 0 else line + hop
+                hop_copy(st, c, hop, way, at).wait_recv()
+
+    def hop_relay(st, c, hop):
+        hop_get(st, c, hop)
+        if hop < lines - 1:
+            hop_send(st, c, hop + 1)
+
     def share(st, c):
-        block = held[st][c].at[own]
-        line_copies[st, c] = [
-            send(block, block, zs.at[st, c, k], zr.at[st, c, k], (p, row))
-            for k, p in enumerate(line_peers)
-        ]
+        block = block_at(st, c, line)
+        hop_send(st, c, 1)
         row_copies[st, c] = [
             send(
                 block,
@@ -202,6 +286,8 @@
         held[st][c][line * n_aux + a, part] = b
         full[st][a, part, own_rows(c), :] = b
 
+    for f in fetched:
+        f.wait()
     for c in range(CHUNKS):
 
         @pl.loop(0, n_aux)
@@ -211,6 +297,8 @@
 
         share(0, c)
 
+    ham = ham_ref[...]
+    energy_ref[...] = 0.5 * (ham + ham.T)
     energy = energy_ref[...]
     e_hi = energy.astype(jnp.bfloat16)
     e_right[:, :width] = e_hi
@@ -242,9 +330,30 @@
         zero = jnp.zeros((rows, width), jnp.float32)
         lax.fori_loop(0, half, body, (zero, zero), unroll=4)
 
-    for st in range(STAGES):
-        for c in range(CHUNKS):
+    steps = [(st, c) for st in range(STAGES) for c in range(CHUNKS)]
+    hop_relay(0, 0, 1)
+    for n, (st, c) in enumerate(steps):
+        if st >= 0:
             cut = slice(c * rows, (c + 1) * rows)
+            if lines > 2:
+                hop_relay(st, c, 2)
+            own = pl.ds(pl.multiple_of(line * n_aux, n_aux), n_aux)
+            flat = held[st][c][own].reshape(n_aux * 2 * rows, width)
+            both = jnp.dot(flat, e_right[...], preferred_element_type=jnp.float32)
+            right[...] = (both[:, :width] + both[:, width:]).reshape(n_aux, 2, rows, width)
+            for hop in range(3, lines):
+                hop_relay(st, c, hop)
+
+            gather_sum(st, c, 0)
+
+            @pl.loop(0, n_aux)
+            def _(a, st=st, c=c):
+                give[st][c][a] = run[last_ref[a]].astype(jnp.bfloat16)
+
+            across = send(give[st][c], take[st][c], ys.at[st, c], yr.at[st, c], (beside, row))
+            gather_sum(st, c, 1)
+            if n + 1 < len(steps):
+                hop_relay(*steps[n + 1], 1)
             if c == 0:
                 for cc in range(CHUNKS):
                     for d in row_copies[st, cc]:
@@ -258,20 +367,6 @@
                         )
                         left[a, part] = both[:rows_dev] + both[rows_dev:]
 
-            flat = held[st][c][own].reshape(n_aux * 2 * rows, width)
-            both = jnp.dot(flat, e_right[...], preferred_element_type=jnp.float32)
-            right[...] = (both[:, :width] + both[:, width:]).reshape(n_aux, 2, rows, width)
-
-            for d in line_copies[st, c]:
-                d.wait_recv()
-            gather_sum(st, c, 0)
-
-            @pl.loop(0, n_aux)
-            def _(a, st=st, c=c):
-                give[st][c][a] = run[last_ref[a]].astype(jnp.bfloat16)
-
-            across = send(give[st][c], take[st][c], ys.at[st, c], yr.at[st, c], (beside, row))
-            gather_sum(st, c, 1)
             across.wait_recv()
 
             weight = step_size / 6.0 * (1.0 if st in (0, STAGES - 1) else 2.0)
@@ -309,10 +404,17 @@
 
     for d in copies:
         d.wait_send()
+    for st, c in steps:
+        for hop in range(1, lines):
+            for way in range(2):
+
+                @pl.when(hop_sends(hop, way))
+                def _(st=st, c=c, hop=hop, way=way):
+                    at = line - (hop - 1) if way == 0 else line + (hop - 1)
+                    hop_copy(st, c, hop, way, at).wait_send()
 
 
 def by_states(rho_real, rho_imag, hamiltonian, damping, couplings, mode_vector, mode_coef):
-    energy = 0.5 * (hamiltonian + hamiltonian.T)
     n_aux, rows_dev, width = rho_real.shape
     per_aux = couplings.shape[2]
     devices = lax.axis_size("aux")
@@ -324,13 +426,26 @@
     row = lax.axis_index("row")
     line, side = aux // 2, aux % 2
 
-    every = lax.all_gather(couplings, "aux", axis=0, tiled=True)
-    every = every.reshape(lines, 2, n_aux, 3, per_aux)
-    every = lax.dynamic_index_in_dim(every, side, 1, keepdims=False)
-    count = lines * n_aux * per_aux
-    targets = every[:, :, 0, :].reshape(count)
-    modes = every[:, :, 1, :].reshape(count)
-    weights = every[:, :, 2, :].reshape(count)
+    smem = pl.BlockSpec(memory_space=pltpu.SMEM)
+    vmem = pl.BlockSpec(memory_space=pltpu.VMEM)
+    anywhere = pl.BlockSpec(memory_space=pl.ANY)
+    dma = pltpu.SemaphoreType.DMA
+    local = n_aux * per_aux
+    lanes = -(-local // 128) * 128
+    packed = couplings.transpose(1, 0, 2).reshape(3, local)
+    packed = jnp.pad(packed, ((0, 5), (0, lanes - local)))
+    every = pl.pallas_call(
+        functools.partial(swap_kernel, lines),
+        out_shape=jax.ShapeDtypeStruct((lines, 8, lanes), jnp.int32),
+        in_specs=[vmem],
+        out_specs=vmem,
+        scratch_shapes=[dma, dma((lines - 1,)), dma((lines - 1,))],
+        compiler_params=pltpu.CompilerParams(collective_id=1, has_side_effects=True),
+    )(packed)
+    count = lines * local
+    targets = every[:, 0, :local].reshape(count)
+    modes = every[:, 1, :local].reshape(count)
+    weights = every[:, 2, :local].reshape(count)
     order = jnp.arange(count)
     sources = order // per_aux
     dest = targets // n_aux
@@ -374,17 +489,17 @@
     fac_imag = -minus[:, None, None] * (row_vec[:, :, None] - vectors[:, None, :])
 
     rows = rows_dev // CHUNKS
-    smem = pl.BlockSpec(memory_space=pltpu.SMEM)
-    vmem = pl.BlockSpec(memory_space=pltpu.VMEM)
     bf16, f32 = jnp.bfloat16, jnp.float32
     piece = pltpu.VMEM((n_aux, 2, rows, width), bf16)
-    dma = pltpu.SemaphoreType.DMA
     grid = (STAGES, CHUNKS)
     scratch = (
         [pltpu.VMEM((lines * n_aux, 2, rows, width), bf16)] * (STAGES * CHUNKS)
         + [pltpu.VMEM((n_aux, 2, row_devs * rows_dev, width), bf16)] * STAGES
         + [piece] * (2 * STAGES * CHUNKS)
         + [
+            pltpu.VMEM((n_aux, rows_dev, width), f32),
+            pltpu.VMEM((n_aux, rows_dev, width), f32),
+            pltpu.VMEM((width, width), f32),
             pltpu.VMEM((half + 1, 2, rows, width), f32),
             pltpu.VMEM((n_aux, 2, rows_dev, width), f32),
             pltpu.VMEM((n_aux, 2, rows_dev, width), f32),
@@ -392,25 +507,26 @@
             pltpu.VMEM((n_aux, 2, rows, width), f32),
             pltpu.VMEM((2 * rows_dev, width), bf16),
             pltpu.VMEM((width, 2 * width), bf16),
-            dma(grid + (lines - 1,)),
-            dma(grid + (lines - 1,)),
+            dma(grid + (2, lines - 1)),
+            dma(grid + (2, lines - 1)),
             dma(grid + (row_devs - 1,)),
             dma(grid + (row_devs - 1,)),
             dma(grid),
             dma(grid),
+            dma((2,)),
         ]
     )
     shape = jax.ShapeDtypeStruct((n_aux, rows_dev, width), f32)
     return pl.pallas_call(
         functools.partial(kernel, lines, row_devs, half),
         out_shape=(shape, shape),
-        in_specs=[smem] * 4 + [vmem] * 5,
+        in_specs=[smem] * 4 + [anywhere] * 2 + [vmem] * 3,
         out_specs=(vmem, vmem),
         scratch_shapes=scratch,
         compiler_params=pltpu.CompilerParams(
             collective_id=0, has_side_effects=True, vmem_limit_bytes=40 * 1024 * 1024
         ),
-    )(src, keep, last, damping, rho_real, rho_imag, energy, fac_real, fac_imag)
+    )(src, keep, last, damping, rho_real, rho_imag, hamiltonian, fac_real, fac_imag)
 
 
 def solution(mesh):

time: 153 us -> 103 us (0.67)
  the two profiles are of different devices: /device:TPU:25 before, /device:TPU:0 now
where the time goes in v2:
time: 103 us
  Pallas kernels  94.5 us (92%)
  local copies, waits for them, and re-layouts  4.33 us (4%)
  other arithmetic  1.82 us (2%)
  matrix products  1.09 us (1%)
    pallas_call x1, Pallas kernels, by_states(): pl.pallas_call(functools.partial(kernel, lines, row_devs, half), out_shap...  86 us
    pallas_call x1, Pallas kernels, by_states(): pl.pallas_call(functools.partial(swap_kernel, lines), out_shape=jax.Shape...  8.58 us

profile of v2, /device:TPU:0, one launch (start us, length us, event | category | flops | bytes accessed | tf_op | source)
XLA Modules:
  0.0 102.5 jit_solution(4772659638622438166)
XLA Ops:
  0.6 0.0 copy-start
  0.7 0.8 copy.11
  1.5 0.1 reshape.289
  1.6 0.6 pad.4.mine_ref
  2.2 8.6 %shard_map.86 = s32[4,8,128]{2,1,0:T(8,128)} custom-call(s32[8,128]{1,0:T(8,128)} %pad.4.mine_ref), custom_call_target="tpu_custom_call" | custom-call | tf_op jit(solution)/shard_map/pallas_call | solution.py:437
  10.8 0.9 slice_reduce_fusion.1
  11.6 0.1 broadcast_in_dim.84
  11.7 0.1 broadcast_in_dim.86
  11.8 0.1 reshape_squeeze.3
  11.9 0.1 fusion.5
  12.0 0.2 convert_reduce_fusion.1
  12.2 0.4 convert_reduce_fusion
  12.6 0.2 select_reduce_fusion.1
  12.8 0.1 and_convert_fusion.keep_ref
  12.9 0.9 fusion.4
  13.7 0.1 fusion.19
  13.8 0.0 copy-done
  13.8 0.2 fusion.3
  14.0 0.1 constant_dynamic-slice_fusion
  14.1 0.0 copy-start.1
  14.1 0.0 copy-start.2
  14.1 0.0 copy-start.3
  14.1 0.0 copy-start.4
  14.2 0.8 subtract_multiply_fusion
  14.9 0.1 copy-done.1
  15.1 0.1 copy-done.2
  15.2 0.0 copy-done.3
  15.2 0.0 copy-done.4
  15.2 86.0 %shard_map.87 = (f32[16,32,128]{2,1,0:T(8,128)S(1)}, f32[16,32,128]{2,1,0:T(8,128)S(1)}) custom-call(s32[96]{0:T(128)S(1)} %get-tuple-element.9.src_ref, f32[96]{0:T(128)S(1)} %and_convert_fusion.keep_ref, s32[32]{0:T(128)S(1)} %broadcast_select_fusion.last_ref, f32[16]{0:T(128)S(1)} %copy-done.4, f32[16,32,128]{2,1,0:T(8,128)S(1)} %copy-done.1, ...), custom_call_target="tpu_custom_call" | custom-call | tf_op jit(solution)/shard_map/pallas_call | solution.py:520
  101.1 0.7 copy.14
  101.8 0.7 copy.15
  (6 shorter events, 0.0 us)
Async XLA Ops:
  0.6 13.2 %copy-start = (f32[128,128]{1,0:T(8,128)S(1)}, f32[128,128]{1,0:T(8,128)}, u32[]{:S(2)}) copy-start(f32[128,128]{1,0:T(8,128)} %param.12) | copy-start | bytes 196612
  14.1 1.0 copy-start.1
  14.1 1.0 %copy-start.2 = (f32[16,32,128]{2,1,0:T(8,128)S(1)}, f32[16,32,128]{2,1,0:T(8,128)}, u32[]{:S(2)}) copy-start(f32[16,32,128]{2,1,0:T(8,128)} %imag_in.1) | copy-start | bytes 786436
  14.1 1.0 %copy-start.3 = (f32[128,128]{1,0:T(8,128)S(1)}, f32[128,128]{1,0:T(8,128)}, u32[]{:S(2)}) copy-start(f32[128,128]{1,0:T(8,128)} %ham_ref.1) | copy-start | bytes 196612
  14.1 1.0 copy-start.4

commit v3 on v2

--- a/solution.py
+++ b/solution.py
@@ -120,47 +120,19 @@
     return (state_real, state_imag)
 
 
-def swap_kernel(lines, mine_ref, all_ref, local_sem, send_sem, recv_sem):
-    aux = lax.axis_index("aux")
-    row = lax.axis_index("row")
-    line = aux // 2
-    peers = [(lax.rem(aux + 2 * k, 2 * lines), row) for k in range(1, lines)]
-    keep = pltpu.make_async_copy(mine_ref, all_ref.at[line], local_sem)
-    keep.start()
-    barrier = pltpu.get_barrier_semaphore()
-    for p in peers:
-        pl.semaphore_signal(barrier, inc=1, device_id=p, device_id_type=MESH)
-    pl.semaphore_wait(barrier, len(peers))
-    copies = []
-    for k, p in enumerate(peers):
-        c = pltpu.make_async_remote_copy(
-            src_ref=mine_ref,
-            dst_ref=all_ref.at[line],
-            send_sem=send_sem.at[k],
-            recv_sem=recv_sem.at[k],
-            device_id=p,
-            device_id_type=MESH,
-        )
-        c.start()
-        copies.append(c)
-    keep.wait()
-    for c in copies:
-        c.wait()
-
-
 def kernel(
     lines,
     row_devs,
     half,
-    src_ref,
-    keep_ref,
-    last_ref,
+    count,
+    links_per,
     rate_ref,
+    coef_ref,
     real_in,
     imag_in,
     ham_ref,
-    facr_ref,
-    faci_ref,
+    mode_ref,
+    link_ref,
     outr_ref,
     outi_ref,
     *scratch,
@@ -172,8 +144,10 @@
     full = [scratch.pop(0) for _ in range(STAGES)]
     give = [[scratch.pop(0) for _ in range(CHUNKS)] for _ in range(STAGES)]
     take = [[scratch.pop(0) for _ in range(CHUNKS)] for _ in range(STAGES)]
-    real_ref, imag_ref, energy_ref = scratch[:3]
-    run, now, total, left, right, e_left, e_right, zs, zr, rs, rr, ys, yr, ins = scratch[3:]
+    real_ref, imag_ref, energy_ref, facr_ref, faci_ref, turned, lists, plan = scratch[:8]
+    links = scratch[8 : 8 + lines]
+    run, now, total, left, right, e_left, e_right = scratch[8 + lines : 15 + lines]
+    zs, zr, rs, rr, ys, yr, ls, lr, ins = scratch[15 + lines :]
 
     fetched = [
         pltpu.make_async_copy(real_in, real_ref, ins.at[0]),
@@ -185,24 +159,18 @@
     aux = lax.axis_index("aux")
     row = lax.axis_index("row")
     line = aux // 2
-    beside = aux + 1 - 2 * lax.rem(aux, 2)
+    side = lax.rem(aux, 2)
+    beside = aux + 1 - 2 * side
     row_peers = [lax.rem(row + k, row_devs) for k in range(1, row_devs)]
     last_line = lines - 1
 
     barrier = pltpu.get_barrier_semaphore()
 
-    @pl.when(line < last_line)
-    def _():
-        pl.semaphore_signal(barrier, inc=1, device_id=(aux + 2, row), device_id_type=MESH)
-
-    @pl.when(line > 0)
-    def _():
-        pl.semaphore_signal(barrier, inc=1, device_id=(aux - 2, row), device_id_type=MESH)
-
-    for p in [(beside, row)] + [(aux, p) for p in row_peers]:
+    line_peers = [lax.rem(aux + 2 * k, 2 * lines) for k in range(1, lines)]
+    peers = [(p, row) for p in line_peers + [beside]] + [(aux, p) for p in row_peers]
+    for p in peers:
         pl.semaphore_signal(barrier, inc=1, device_id=p, device_id_type=MESH)
-    ends = (line == 0).astype(jnp.int32) + (line == last_line).astype(jnp.int32)
-    pl.semaphore_wait(barrier, 2 + row_devs - ends)
+    pl.semaphore_wait(barrier, len(peers))
 
     copies = []
 
@@ -286,6 +254,10 @@
         held[st][c][line * n_aux + a, part] = b
         full[st][a, part, own_rows(c), :] = b
 
+    link_copies = [
+        send(link_ref, links[k], ls.at[k - 1], lr.at[k - 1], (p, row))
+        for k, p in enumerate(line_peers, 1)
+    ]
     for f in fetched:
         f.wait()
     for c in range(CHUNKS):
@@ -309,14 +281,89 @@
     e_left[rows_dev:] = (mine - m_hi.astype(jnp.float32)).astype(jnp.bfloat16)
     run[0] = jnp.zeros(run.shape[1:], jnp.float32)
 
+    turned[...] = mode_ref[...].T
+    links[0][...] = link_ref[...]
+    for d in link_copies:
+        d.wait_recv()
+    lanes = link_ref.shape[1]
+    i32 = jnp.int32
+    lane = lax.broadcasted_iota(i32, (1, lanes), 1)
+    diagonal = lax.broadcasted_iota(i32, (lanes, lanes), 0) == lax.broadcasted_iota(
+        i32, (lanes, lanes), 1
+    )
+    far = 1 << 20
+    keys_row, modes_row, weights_row, source_row, keys_col = [], [], [], [], []
+    for k in range(lines):
+        from_line = lax.rem(line - k + lines, lines)
+        target = links[k][0:1, :]
+        dest = target // n_aux
+        chosen = (dest // 2 == line) & (lane < count)
+        group = jnp.where(lax.rem(dest, 2) == side, 1, 0)
+        key = group * n_aux + lax.rem(target, n_aux)
+        place_in = from_line * lanes + lane
+        key = jnp.where(chosen, key * (lines * lanes) + place_in, far)
+        keys_row.append(key)
+        modes_row.append(links[k][1:2, :])
+        weights_row.append(links[k][2:3, :])
+        source_row.append(from_line * n_aux + lane // links_per)
+        keys_col.append(jnp.sum(jnp.where(diagonal, key, 0), axis=1, keepdims=True))
+    span = lines * lanes
+    key = jnp.concatenate(keys_row, axis=1)
+    column = jnp.concatenate(keys_col, axis=0)
+    chosen = key < far
+    before = column < key
+    rank = jnp.sum(jnp.where(before, 1, 0), axis=0, keepdims=True)
+    again = jnp.sum(jnp.where(before & (column // span == key // span), 1, 0), axis=0, keepdims=True)
+    second = n_aux * span
+    first_count = jnp.sum(jnp.where(key < second, 1, 0), axis=1, keepdims=True)
+    ranked = jnp.where(key < second, rank, rank - first_count)
+    slot = jnp.where(key < second, ranked, ranked + half)
+    slot = jnp.where(chosen & (ranked < half), slot, -1)
+    pick = lax.broadcasted_iota(i32, (2 * half, span), 0) == slot
+
+    def picked(values):
+        return jnp.sum(jnp.where(pick, values, 0), axis=1, keepdims=True)
+
+    at = lax.broadcasted_iota(i32, (2 * half, 128), 1)
+    table = jnp.where(at == 0, picked(jnp.concatenate(source_row, axis=1)), 0)
+    table = jnp.where(at == 1, picked(jnp.concatenate(modes_row, axis=1)), table)
+    table = jnp.where(at == 2, picked(jnp.concatenate(weights_row, axis=1)), table)
+    table = jnp.where(at == 3, picked(jnp.where(again > 0, 1, 0)), table)
+    table = jnp.where(at == 4, picked(jnp.ones_like(key)), table)
+    lists[: 2 * half] = table
+    wanted = lax.broadcasted_iota(i32, (2 * n_aux, span), 0)
+    upto = jnp.sum(jnp.where(key < (wanted + 1) * span, 1, 0), axis=1, keepdims=True)
+    here = jnp.sum(jnp.where(key // span == wanted, 1, 0), axis=1, keepdims=True)
+    tall = lax.broadcasted_iota(i32, (2 * n_aux, 1), 0)
+    upto = jnp.minimum(jnp.where(tall < n_aux, upto, upto - first_count), half)
+    lists[2 * half :] = jnp.broadcast_to(jnp.where(here > 0, upto, 0), (2 * n_aux, 128))
+    planned = pltpu.make_async_copy(lists, plan, ins.at[2])
+    planned.start()
+    planned.wait()
+
+    mode_lane = lax.broadcasted_iota(i32, (rows_dev, mode_ref.shape[0]), 1)
+
+    @pl.loop(0, 2 * half)
+    def _(e):
+        m = plan[e, 1]
+        w = plan[e, 2]
+        scaled = w.astype(jnp.float32)
+        plus = scaled * coef_ref[1, m]
+        minus = jnp.where(w == 0, plan[e, 4].astype(jnp.float32), scaled * coef_ref[0, m])
+        across = mode_ref[pl.ds(m, 1), :]
+        mine = turned[pl.ds(pl.multiple_of(row * rows_dev, rows_dev), rows_dev), :]
+        down = jnp.sum(jnp.where(mode_lane == m, mine, 0.0), axis=1, keepdims=True)
+        facr_ref[e] = plus * (down + across)
+        faci_ref[e] = -minus * (down - across)
+
     def gather_sum(st, c, group):
         cut = slice(c * rows, (c + 1) * rows)
 
         def body(e, acc):
             ar, ai = acc
             i = group * half + e
-            s = src_ref[i]
-            keep = keep_ref[i]
+            s = plan[i, 0]
+            keep = plan[i, 3].astype(jnp.float32)
             xr = held[st][c][s, 0].astype(jnp.float32)
             xi = held[st][c][s, 1].astype(jnp.float32)
             fr = facr_ref[i, cut, :]
@@ -333,74 +380,73 @@
     steps = [(st, c) for st in range(STAGES) for c in range(CHUNKS)]
     hop_relay(0, 0, 1)
     for n, (st, c) in enumerate(steps):
-        if st >= 0:
-            cut = slice(c * rows, (c + 1) * rows)
-            if lines > 2:
-                hop_relay(st, c, 2)
-            own = pl.ds(pl.multiple_of(line * n_aux, n_aux), n_aux)
-            flat = held[st][c][own].reshape(n_aux * 2 * rows, width)
-            both = jnp.dot(flat, e_right[...], preferred_element_type=jnp.float32)
-            right[...] = (both[:, :width] + both[:, width:]).reshape(n_aux, 2, rows, width)
-            for hop in range(3, lines):
-                hop_relay(st, c, hop)
-
-            gather_sum(st, c, 0)
+        cut = slice(c * rows, (c + 1) * rows)
+        if lines > 2:
+            hop_relay(st, c, 2)
+        own = pl.ds(pl.multiple_of(line * n_aux, n_aux), n_aux)
+        flat = held[st][c][own].reshape(n_aux * 2 * rows, width)
+        both = jnp.dot(flat, e_right[...], preferred_element_type=jnp.float32)
+        right[...] = (both[:, :width] + both[:, width:]).reshape(n_aux, 2, rows, width)
+        for hop in range(3, lines):
+            hop_relay(st, c, hop)
+
+        gather_sum(st, c, 0)
+
+        @pl.loop(0, n_aux)
+        def _(a, st=st, c=c):
+            give[st][c][a] = run[plan[2 * half + a, 0]].astype(jnp.bfloat16)
+
+        across = send(give[st][c], take[st][c], ys.at[st, c], yr.at[st, c], (beside, row))
+        gather_sum(st, c, 1)
+        if n + 1 < len(steps):
+            hop_relay(*steps[n + 1], 1)
+        if c == 0:
+            for cc in range(CHUNKS):
+                for d in row_copies[st, cc]:
+                    d.wait_recv()
 
             @pl.loop(0, n_aux)
-            def _(a, st=st, c=c):
-                give[st][c][a] = run[last_ref[a]].astype(jnp.bfloat16)
-
-            across = send(give[st][c], take[st][c], ys.at[st, c], yr.at[st, c], (beside, row))
-            gather_sum(st, c, 1)
-            if n + 1 < len(steps):
-                hop_relay(*steps[n + 1], 1)
-            if c == 0:
-                for cc in range(CHUNKS):
-                    for d in row_copies[st, cc]:
-                        d.wait_recv()
-
-                @pl.loop(0, n_aux)
-                def _(a, st=st):
-                    for part in range(2):
-                        both = jnp.dot(
-                            e_left[...], full[st][a, part], preferred_element_type=jnp.float32
-                        )
-                        left[a, part] = both[:rows_dev] + both[rows_dev:]
-
-            across.wait_recv()
-
-            weight = step_size / 6.0 * (1.0 if st in (0, STAGES - 1) else 2.0)
-            ahead = step_size if st == STAGES - 2 else 0.5 * step_size
-
-            @pl.loop(0, n_aux)
-            def _(a, st=st, c=c, cut=cut, weight=weight, ahead=ahead):
-                came = run[last_ref[n_aux + a]] + take[st][c][a].astype(jnp.float32)
-                prod_r = left[a, 0, cut, :] - right[a, 0]
-                prod_i = left[a, 1, cut, :] - right[a, 1]
-                rate = rate_ref[a]
-                base_r = real_ref[a, cut, :]
-                base_i = imag_ref[a, cut, :]
-                now_r = base_r if st == 0 else now[a, 0, cut, :]
-                now_i = base_i if st == 0 else now[a, 1, cut, :]
-                k_r = prod_i - rate * now_r + came[0]
-                k_i = came[1] - prod_r - rate * now_i
-                tot_r = (base_r if st == 0 else total[a, 0, cut, :]) + weight * k_r
-                tot_i = (base_i if st == 0 else total[a, 1, cut, :]) + weight * k_i
-                if st == STAGES - 1:
-                    outr_ref[a, cut, :] = tot_r
-                    outi_ref[a, cut, :] = tot_i
-                else:
-                    total[a, 0, cut, :] = tot_r
-                    total[a, 1, cut, :] = tot_i
-                    next_r = base_r + ahead * k_r
-                    next_i = base_i + ahead * k_i
-                    now[a, 0, cut, :] = next_r
-                    now[a, 1, cut, :] = next_i
-                    place(st + 1, c, a, 0, next_r)
-                    place(st + 1, c, a, 1, next_i)
-
-            if st < STAGES - 1:
-                share(st + 1, c)
+            def _(a, st=st):
+                for part in range(2):
+                    both = jnp.dot(
+                        e_left[...], full[st][a, part], preferred_element_type=jnp.float32
+                    )
+                    left[a, part] = both[:rows_dev] + both[rows_dev:]
+
+        across.wait_recv()
+
+        weight = step_size / 6.0 * (1.0 if st in (0, STAGES - 1) else 2.0)
+        ahead = step_size if st == STAGES - 2 else 0.5 * step_size
+
+        @pl.loop(0, n_aux)
+        def _(a, st=st, c=c, cut=cut, weight=weight, ahead=ahead):
+            came = run[plan[2 * half + n_aux + a, 0]] + take[st][c][a].astype(jnp.float32)
+            prod_r = left[a, 0, cut, :] - right[a, 0]
+            prod_i = left[a, 1, cut, :] - right[a, 1]
+            rate = rate_ref[a]
+            base_r = real_ref[a, cut, :]
+            base_i = imag_ref[a, cut, :]
+            now_r = base_r if st == 0 else now[a, 0, cut, :]
+            now_i = base_i if st == 0 else now[a, 1, cut, :]
+            k_r = prod_i - rate * now_r + came[0]
+            k_i = came[1] - prod_r - rate * now_i
+            tot_r = (base_r if st == 0 else total[a, 0, cut, :]) + weight * k_r
+            tot_i = (base_i if st == 0 else total[a, 1, cut, :]) + weight * k_i
+            if st == STAGES - 1:
+                outr_ref[a, cut, :] = tot_r
+                outi_ref[a, cut, :] = tot_i
+            else:
+                total[a, 0, cut, :] = tot_r
+                total[a, 1, cut, :] = tot_i
+                next_r = base_r + ahead * k_r
+                next_i = base_i + ahead * k_i
+                now[a, 0, cut, :] = next_r
+                now[a, 1, cut, :] = next_i
+                place(st + 1, c, a, 0, next_r)
+                place(st + 1, c, a, 1, next_i)
+
+        if st < STAGES - 1:
+            share(st + 1, c)
 
     for d in copies:
         d.wait_send()
@@ -422,71 +468,14 @@
     lines = devices // 2
     slots = max(1, -(-n_aux * per_aux // devices))
     half = lines * slots
-    aux = lax.axis_index("aux")
-    row = lax.axis_index("row")
-    line, side = aux // 2, aux % 2
-
     smem = pl.BlockSpec(memory_space=pltpu.SMEM)
     vmem = pl.BlockSpec(memory_space=pltpu.VMEM)
     anywhere = pl.BlockSpec(memory_space=pl.ANY)
     dma = pltpu.SemaphoreType.DMA
-    local = n_aux * per_aux
-    lanes = -(-local // 128) * 128
-    packed = couplings.transpose(1, 0, 2).reshape(3, local)
-    packed = jnp.pad(packed, ((0, 5), (0, lanes - local)))
-    every = pl.pallas_call(
-        functools.partial(swap_kernel, lines),
-        out_shape=jax.ShapeDtypeStruct((lines, 8, lanes), jnp.int32),
-        in_specs=[vmem],
-        out_specs=vmem,
-        scratch_shapes=[dma, dma((lines - 1,)), dma((lines - 1,))],
-        compiler_params=pltpu.CompilerParams(collective_id=1, has_side_effects=True),
-    )(packed)
-    count = lines * local
-    targets = every[:, 0, :local].reshape(count)
-    modes = every[:, 1, :local].reshape(count)
-    weights = every[:, 2, :local].reshape(count)
-    order = jnp.arange(count)
-    sources = order // per_aux
-    dest = targets // n_aux
-    chosen = dest // 2 == line
-    group = (dest % 2 == side).astype(jnp.int32)
-    key = jnp.where(chosen, group * n_aux + targets % n_aux, 2 * n_aux)
-    before = (key[None, :] < key[:, None]) | (
-        (key[None, :] == key[:, None]) & (order[None, :] < order[:, None])
-    )
-    same_group = chosen[None, :] & (group[None, :] == group[:, None])
-    ranked = jnp.sum((before & same_group).astype(jnp.int32), axis=1)
-    slot_of = jnp.where(chosen, group * half + ranked, -1)
-    pick = slot_of[None, :] == jnp.arange(2 * half)[:, None]
-
-    def picked(values):
-        return jnp.sum(jnp.where(pick, values[None, :], 0), axis=1)
-
-    src = picked(sources)
-    mode = picked(modes)
-    weight = picked(weights)
-    filled = picked(jnp.ones_like(order))
-    at_key = picked(key) + (1 - filled) * (2 * n_aux)
-    previous = jnp.concatenate([jnp.full((1,), -1, at_key.dtype), at_key[:-1]])
-    first = jnp.arange(2 * half) % half == 0
-    keep = ((at_key == previous) & ~first).astype(jnp.float32)
-    wanted = jnp.arange(2 * n_aux)
-    in_group = chosen[None, :] & (group[None, :] == wanted[:, None] // n_aux)
-    upto = jnp.sum((in_group & (key[None, :] <= wanted[:, None])).astype(jnp.int32), axis=1)
-    any_here = jnp.any(key[None, :] == wanted[:, None], axis=1)
-    last = jnp.where(any_here, upto, 0)
-
-    picker = (mode[:, None] == jnp.arange(mode_vector.shape[0])[None, :]).astype(jnp.float32)
-    vectors = jnp.dot(picker, mode_vector, precision=high, preferred_element_type=jnp.float32)
-    coefs = jnp.dot(picker, mode_coef.T, precision=high, preferred_element_type=jnp.float32)
-    scaled = weight.astype(jnp.float32)
-    there = filled.astype(jnp.float32)
-    plus = there * scaled * coefs[:, 1]
-    minus = there * jnp.where(weight == 0, 1.0, scaled * coefs[:, 0])
-    row_vec = lax.dynamic_slice_in_dim(vectors, row * rows_dev, rows_dev, 1)
-    fac_real = plus[:, None, None] * (row_vec[:, :, None] + vectors[:, None, :])
-    fac_imag = -minus[:, None, None] * (row_vec[:, :, None] - vectors[:, None, :])
+    count = n_aux * per_aux
+    lanes = -(-count // 128) * 128
+    packed = couplings.transpose(1, 0, 2).reshape(3, count)
+    packed = jnp.pad(packed, ((0, 5), (0, lanes - count)))
 
     rows = rows_dev // CHUNKS
     bf16, f32 = jnp.bfloat16, jnp.float32
@@ -500,6 +489,14 @@
             pltpu.VMEM((n_aux, rows_dev, width), f32),
             pltpu.VMEM((n_aux, rows_dev, width), f32),
             pltpu.VMEM((width, width), f32),
+            pltpu.VMEM((2 * half, rows_dev, width), f32),
+            pltpu.VMEM((2 * half, rows_dev, width), f32),
+            pltpu.VMEM((width, mode_vector.shape[0]), f32),
+            pltpu.VMEM((2 * half + 2 * n_aux, 128), jnp.int32),
+            pltpu.SMEM((2 * half + 2 * n_aux, 128), jnp.int32),
+        ]
+        + [pltpu.VMEM((8, lanes), jnp.int32)] * lines
+        + [
             pltpu.VMEM((half + 1, 2, rows, width), f32),
             pltpu.VMEM((n_aux, 2, rows_dev, width), f32),
             pltpu.VMEM((n_aux, 2, rows_dev, width), f32),
@@ -513,20 +510,22 @@
             dma(grid + (row_devs - 1,)),
             dma(grid),
             dma(grid),
-            dma((2,)),
+            dma((lines - 1,)),
+            dma((lines - 1,)),
+            dma((3,)),
         ]
     )
     shape = jax.ShapeDtypeStruct((n_aux, rows_dev, width), f32)
     return pl.pallas_call(
-        functools.partial(kernel, lines, row_devs, half),
+        functools.partial(kernel, lines, row_devs, half, count, per_aux),
         out_shape=(shape, shape),
-        in_specs=[smem] * 4 + [anywhere] * 2 + [vmem] * 3,
+        in_specs=[smem] * 2 + [anywhere] * 2 + [vmem] * 3,
         out_specs=(vmem, vmem),
         scratch_shapes=scratch,
         compiler_params=pltpu.CompilerParams(
             collective_id=0, has_side_effects=True, vmem_limit_bytes=40 * 1024 * 1024
         ),
-    )(src, keep, last, damping, rho_real, rho_imag, hamiltonian, fac_real, fac_imag)
+    )(damping, mode_coef, rho_real, rho_imag, hamiltonian, mode_vector, packed)
 
 
 def solution(mesh):

time: 103 us -> 101 us (0.981)
  other arithmetic: 1.82 us -> 0 us
  local copies, waits for them, and re-layouts: 4.33 us -> 5.72 us
  matrix products: 1.09 us -> 0 us
    unnamed x12 -> x14, local copies, waits for them, and re-layouts: 1.65 us -> 4.8 us
    dot_general x2 -> x0, matrix products: 1.09 us -> none  [the longest x1 0.86 us: by_states(): jnp.dot(picker, mode_coef.T, precision=high, preferred_element_type=jnp.f...]
    pallas_call x2 -> x1, Pallas kernels: 94.5 us -> 94.1 us  [by_states(): pl.pallas_call(functools.partial(kernel, lines, row_devs, half, count, pe...]
where the time goes in v3:
time: 101 us; the launch traced here: 100 us
  Pallas kernels  94.1 us (93%)
  local copies, waits for them, and re-layouts  5.72 us (6%)
    pallas_call x1, Pallas kernels, by_states(): pl.pallas_call(functools.partial(kernel, lines, row_devs, half, count, pe...  94.1 us
    unnamed x14, local copies, waits for them, and re-layouts  4.8 us

profile of v3, /device:TPU:0, one launch (start us, length us, event | category | flops | bytes accessed | tf_op | source)
XLA Modules:
  0.0 100.5 jit_solution(8963130111789152671)
XLA Ops:
  0.6 0.0 copy-start.2
  0.6 0.8 copy.10
  1.5 0.1 reshape.7
  1.6 0.0 copy-start.4
  1.6 0.0 copy-start.5
  1.6 0.0 copy-done.2
  1.6 0.6 copy-done.4
  2.2 0.0 copy-done.5
  2.2 0.0 copy-start
  2.2 0.9 copy-done
  3.2 0.0 copy-start.1
  3.2 0.9 copy-done.1
  4.1 0.0 copy-start.3
  4.1 0.8 copy-done.3
  5.0 94.1 %shard_map.86 = (f32[16,32,128]{2,1,0:T(8,128)S(1)}, f32[16,32,128]{2,1,0:T(8,128)S(1)}) custom-call(f32[16]{0:T(128)S(1)} %copy-done.5, f32[2,128]{1,0:T(2,128)S(1)} %copy-done.4, f32[16,32,128]{2,1,0:T(8,128)S(1)} %copy-done, f32[16,32,128]{2,1,0:T(8,128)S(1)} %copy-done.1, f32[128,128]{1,0:T(8,128)S(1)} %copy-done.2, f32[128,128]{1,0:T(8,128)S(1)} %copy-done.3, ...), custom_call_target="tpu_custom_call" | custom-call | tf_op jit(solution)/shard_map/pallas_call | solution.py:519
  99.1 0.7 copy.13
  99.8 0.7 copy.14
  (1 shorter events, 0.0 us)
Async XLA Ops:
  0.6 1.0 copy-start.2
  1.6 0.7 copy-start.4
  1.6 0.7 copy-start.5
  2.2 1.0 copy-start
  3.2 0.9 copy-start.1
  4.1 0.8 copy-start.3

commit v4 on v3

--- a/solution.py
+++ b/solution.py
@@ -262,7 +262,7 @@
         f.wait()
     for c in range(CHUNKS):
 
-        @pl.loop(0, n_aux)
+        @pl.loop(0, n_aux, unroll=8)
         def _(a, c=c):
             for part, ref in enumerate((real_ref, imag_ref)):
                 place(0, c, a, part, ref[a, c * rows : (c + 1) * rows, :])
@@ -339,11 +339,12 @@
     lists[2 * half :] = jnp.broadcast_to(jnp.where(here > 0, upto, 0), (2 * n_aux, 128))
     planned = pltpu.make_async_copy(lists, plan, ins.at[2])
     planned.start()
+    hop_relay(0, 0, 1)
     planned.wait()
 
     mode_lane = lax.broadcasted_iota(i32, (rows_dev, mode_ref.shape[0]), 1)
 
-    @pl.loop(0, 2 * half)
+    @pl.loop(0, 2 * half, unroll=8)
     def _(e):
         m = plan[e, 1]
         w = plan[e, 2]
@@ -375,10 +376,9 @@
             return ar, ai
 
         zero = jnp.zeros((rows, width), jnp.float32)
-        lax.fori_loop(0, half, body, (zero, zero), unroll=4)
+        lax.fori_loop(0, half, body, (zero, zero), unroll=12)
 
     steps = [(st, c) for st in range(STAGES) for c in range(CHUNKS)]
-    hop_relay(0, 0, 1)
     for n, (st, c) in enumerate(steps):
         cut = slice(c * rows, (c + 1) * rows)
         if lines > 2:
@@ -392,7 +392,7 @@
 
         gather_sum(st, c, 0)
 
-        @pl.loop(0, n_aux)
+        @pl.loop(0, n_aux, unroll=8)
         def _(a, st=st, c=c):
             give[st][c][a] = run[plan[2 * half + a, 0]].astype(jnp.bfloat16)
 
@@ -405,7 +405,7 @@
                 for d in row_copies[st, cc]:
                     d.wait_recv()
 
-            @pl.loop(0, n_aux)
+            @pl.loop(0, n_aux, unroll=8)
             def _(a, st=st):
                 for part in range(2):
                     both = jnp.dot(
@@ -418,7 +418,7 @@
         weight = step_size / 6.0 * (1.0 if st in (0, STAGES - 1) else 2.0)
         ahead = step_size if st == STAGES - 2 else 0.5 * step_size
 
-        @pl.loop(0, n_aux)
+        @pl.loop(0, n_aux, unroll=8)
         def _(a, st=st, c=c, cut=cut, weight=weight, ahead=ahead):
             came = run[plan[2 * half + n_aux + a, 0]] + take[st][c][a].astype(jnp.float32)
             prod_r = left[a, 0, cut, :] - right[a, 0]
@@ -523,7 +523,7 @@
         out_specs=(vmem, vmem),
         scratch_shapes=scratch,
         compiler_params=pltpu.CompilerParams(
-            collective_id=0, has_side_effects=True, vmem_limit_bytes=40 * 1024 * 1024
+            collective_id=0, has_side_effects=True, vmem_limit_bytes=60 * 1024 * 1024
         ),
     )(damping, mode_coef, rho_real, rho_imag, hamiltonian, mode_vector, packed)
 

time: 101 us -> 92 us (0.911)
  Pallas kernels: 94.1 us -> 87.2 us
  local copies, waits for them, and re-layouts: 5.72 us -> 3.91 us
    pallas_call x1, Pallas kernels: 94.1 us -> 87.2 us  [by_states(): pl.pallas_call(functools.partial(kernel, lines, row_devs, half, count, pe...]
    unnamed x14 -> x4, local copies, waits for them, and re-layouts: 4.8 us -> 2.42 us
where the time goes in v4:
time: 92 us; the launch traced here: 91.7 us
  Pallas kernels  87.2 us (95%)
  local copies, waits for them, and re-layouts  3.91 us (4%)
    pallas_call x1, Pallas kernels, by_states(): pl.pallas_call(functools.partial(kernel, lines, row_devs, half, count, pe...  87.2 us
    unnamed x4, local copies, waits for them, and re-layouts  2.42 us

profile of v4, /device:TPU:0, one launch (start us, length us, event | category | flops | bytes accessed | tf_op | source)
XLA Modules:
  0.0 91.7 jit_solution(11239216015537012735)
XLA Ops:
  0.6 0.8 copy.10
  1.4 0.1 reshape.7
  1.5 0.6 pad.4.link_ref
  2.1 87.2 %shard_map.86 = (f32[16,32,128]{2,1,0:T(8,128)}, f32[16,32,128]{2,1,0:T(8,128)}) custom-call(f32[16]{0:T(128)} %rate_ref.1, f32[2,128]{1,0:T(2,128)} %coef_ref.1, f32[16,32,128]{2,1,0:T(8,128)} %real_in.1, f32[16,32,128]{2,1,0:T(8,128)} %imag_in.1, f32[128,128]{1,0:T(8,128)} %ham_ref.1, f32[128,128]{1,0:T(8,128)} %mode_ref.1, s32[8,128]{1,0:T(8,128)} %pad.4.link_ref), custom_call_target="tpu_custom_call" | custom-call | tf_op jit(solution)/shard_map/pallas_call | solution.py:519
  89.3 0.0 copy-start
  89.3 1.7 %copy.13 = f32[16,32,128]{2,1,0:T(8,128)} copy(f32[16,32,128]{2,1,0:T(8,128)} %get-tuple-element.4) | data formatting | bytes 524288
  91.0 0.0 copy-done
  91.0 0.7 copy.14
Async XLA Ops:
  89.3 1.7 %copy-start = (f32[16,32,128]{2,1,0:T(8,128)S(1)}, f32[16,32,128]{2,1,0:T(8,128)}, u32[]{:S(2)}) copy-start(f32[16,32,128]{2,1,0:T(8,128)} %get-tuple-element.5) | copy-start | bytes 786436

commit v5 on v4

--- a/solution.py
+++ b/solution.py
@@ -10,7 +10,7 @@
 step_size = 0.1
 high = lax.Precision.HIGHEST
 MESH = pl.DeviceIdType.MESH
-CHUNKS = 2
+CHUNKS = 4
 STAGES = 4
 
 
@@ -139,6 +139,7 @@
 ):
     n_aux, rows_dev, width = outr_ref.shape
     rows = rows_dev // CHUNKS
+    pair = 2 * rows
     scratch = list(scratch)
     held = [[scratch.pop(0) for _ in range(CHUNKS)] for _ in range(STAGES)]
     full = [scratch.pop(0) for _ in range(STAGES)]
@@ -190,7 +191,7 @@
     row_copies = {}
 
     def own_rows(c):
-        return pl.ds(pl.multiple_of(row * rows_dev + c * rows, rows), rows)
+        return pl.ds(pl.multiple_of((row * CHUNKS + c) * pair, pair), pair)
 
     def block_at(st, c, at):
         return held[st][c].at[pl.ds(pl.multiple_of(at * n_aux, n_aux), n_aux)]
@@ -241,7 +242,7 @@
         row_copies[st, c] = [
             send(
                 block,
-                full[st].at[:, :, own_rows(c), :],
+                full[st].at[:, own_rows(c), :],
                 rs.at[st, c, k],
                 rr.at[st, c, k],
                 (aux, p),
@@ -249,10 +250,13 @@
             for k, p in enumerate(row_peers)
         ]
 
-    def place(st, c, a, part, x):
+    def place(st, c, a, x):
         b = x.astype(jnp.bfloat16)
-        held[st][c][line * n_aux + a, part] = b
-        full[st][a, part, own_rows(c), :] = b
+        held[st][c][line * n_aux + a] = b
+        full[st][a, own_rows(c), :] = b
+
+    def base_of(a, cut):
+        return jnp.concatenate([real_ref[a, cut, :], imag_ref[a, cut, :]], axis=0)
 
     link_copies = [
         send(link_ref, links[k], ls.at[k - 1], lr.at[k - 1], (p, row))
@@ -264,8 +268,7 @@
 
         @pl.loop(0, n_aux, unroll=8)
         def _(a, c=c):
-            for part, ref in enumerate((real_ref, imag_ref)):
-                place(0, c, a, part, ref[a, c * rows : (c + 1) * rows, :])
+            place(0, c, a, base_of(a, slice(c * rows, (c + 1) * rows)))
 
         share(0, c)
 
@@ -275,10 +278,34 @@
     e_hi = energy.astype(jnp.bfloat16)
     e_right[:, :width] = e_hi
     e_right[:, width:] = (energy - e_hi.astype(jnp.float32)).astype(jnp.bfloat16)
-    mine = energy_ref[pl.ds(pl.multiple_of(row * rows_dev, rows_dev), rows_dev), :]
-    m_hi = mine.astype(jnp.bfloat16)
-    e_left[:rows_dev] = m_hi
-    e_left[rows_dev:] = (mine - m_hi.astype(jnp.float32)).astype(jnp.bfloat16)
+    i32 = jnp.int32
+
+    def spot(i):
+        return i // pair * rows + lax.rem(i, rows)
+
+    def part_of(i):
+        return lax.rem(i // rows, 2)
+
+    tall = 2 * rows_dev
+    wide = 2 * width
+    take_rows = lax.broadcasted_iota(i32, (tall, width), 1) == row * rows_dev + spot(
+        lax.broadcasted_iota(i32, (tall, width), 0)
+    )
+    put_columns = lax.broadcasted_iota(i32, (width, wide), 0) == spot(
+        lax.broadcasted_iota(i32, (width, wide), 1)
+    )
+    same_part = part_of(lax.broadcasted_iota(i32, (tall, wide), 0)) == part_of(
+        lax.broadcasted_iota(i32, (tall, wide), 1)
+    )
+    ones_rows = jnp.where(take_rows, 1.0, 0.0).astype(jnp.bfloat16)
+    ones_columns = jnp.where(put_columns, 1.0, 0.0).astype(jnp.bfloat16)
+    for k in range(2):
+        piece = e_right[:, k * width : (k + 1) * width]
+        mine = jnp.dot(ones_rows, piece, preferred_element_type=jnp.float32)
+        spread = jnp.dot(
+            mine.astype(jnp.bfloat16), ones_columns, preferred_element_type=jnp.float32
+        )
+        e_left[k * tall : (k + 1) * tall] = jnp.where(same_part, spread, 0.0).astype(jnp.bfloat16)
     run[0] = jnp.zeros(run.shape[1:], jnp.float32)
 
     turned[...] = mode_ref[...].T
@@ -286,7 +313,6 @@
     for d in link_copies:
         d.wait_recv()
     lanes = link_ref.shape[1]
-    i32 = jnp.int32
     lane = lax.broadcasted_iota(i32, (1, lanes), 1)
     diagonal = lax.broadcasted_iota(i32, (lanes, lanes), 0) == lax.broadcasted_iota(
         i32, (lanes, lanes), 1
@@ -334,12 +360,14 @@
     wanted = lax.broadcasted_iota(i32, (2 * n_aux, span), 0)
     upto = jnp.sum(jnp.where(key < (wanted + 1) * span, 1, 0), axis=1, keepdims=True)
     here = jnp.sum(jnp.where(key // span == wanted, 1, 0), axis=1, keepdims=True)
-    tall = lax.broadcasted_iota(i32, (2 * n_aux, 1), 0)
-    upto = jnp.minimum(jnp.where(tall < n_aux, upto, upto - first_count), half)
+    which = lax.broadcasted_iota(i32, (2 * n_aux, 1), 0)
+    upto = jnp.minimum(jnp.where(which < n_aux, upto, upto - first_count), half)
     lists[2 * half :] = jnp.broadcast_to(jnp.where(here > 0, upto, 0), (2 * n_aux, 128))
     planned = pltpu.make_async_copy(lists, plan, ins.at[2])
     planned.start()
-    hop_relay(0, 0, 1)
+    steps = [(st, c) for st in range(STAGES) for c in range(CHUNKS)]
+    hop_relay(*steps[0], 1)
+    hop_relay(*steps[1], 1)
     planned.wait()
 
     mode_lane = lax.broadcasted_iota(i32, (rows_dev, mode_ref.shape[0]), 1)
@@ -365,31 +393,25 @@
             i = group * half + e
             s = plan[i, 0]
             keep = plan[i, 3].astype(jnp.float32)
-            xr = held[st][c][s, 0].astype(jnp.float32)
-            xi = held[st][c][s, 1].astype(jnp.float32)
+            x = held[st][c][s].astype(jnp.float32)
+            xr, xi = x[:rows], x[rows:]
             fr = facr_ref[i, cut, :]
             fi = faci_ref[i, cut, :]
             ar = keep * ar + (fr * xr - fi * xi)
             ai = keep * ai + (fr * xi + fi * xr)
-            run[e + 1, 0] = ar
-            run[e + 1, 1] = ai
+            run[e + 1, :rows] = ar
+            run[e + 1, rows:] = ai
             return ar, ai
 
         zero = jnp.zeros((rows, width), jnp.float32)
         lax.fori_loop(0, half, body, (zero, zero), unroll=12)
 
-    steps = [(st, c) for st in range(STAGES) for c in range(CHUNKS)]
+    hop_relay(*steps[0], 2)
     for n, (st, c) in enumerate(steps):
         cut = slice(c * rows, (c + 1) * rows)
-        if lines > 2:
-            hop_relay(st, c, 2)
-        own = pl.ds(pl.multiple_of(line * n_aux, n_aux), n_aux)
-        flat = held[st][c][own].reshape(n_aux * 2 * rows, width)
-        both = jnp.dot(flat, e_right[...], preferred_element_type=jnp.float32)
-        right[...] = (both[:, :width] + both[:, width:]).reshape(n_aux, 2, rows, width)
+        both_cut = slice(c * pair, (c + 1) * pair)
         for hop in range(3, lines):
             hop_relay(st, c, hop)
-
         gather_sum(st, c, 0)
 
         @pl.loop(0, n_aux, unroll=8)
@@ -397,9 +419,15 @@
             give[st][c][a] = run[plan[2 * half + a, 0]].astype(jnp.bfloat16)
 
         across = send(give[st][c], take[st][c], ys.at[st, c], yr.at[st, c], (beside, row))
+        if n + 1 < len(steps):
+            hop_relay(*steps[n + 1], 2)
+        if n + 2 < len(steps):
+            hop_relay(*steps[n + 2], 1)
+        own = pl.ds(pl.multiple_of(line * n_aux, n_aux), n_aux)
+        flat = held[st][c][own].reshape(n_aux * pair, width)
+        both = jnp.dot(flat, e_right[...], preferred_element_type=jnp.float32)
+        right[...] = (both[:, :width] + both[:, width:]).reshape(n_aux, pair, width)
         gather_sum(st, c, 1)
-        if n + 1 < len(steps):
-            hop_relay(*steps[n + 1], 1)
         if c == 0:
             for cc in range(CHUNKS):
                 for d in row_copies[st, cc]:
@@ -407,11 +435,8 @@
 
             @pl.loop(0, n_aux, unroll=8)
             def _(a, st=st):
-                for part in range(2):
-                    both = jnp.dot(
-                        e_left[...], full[st][a, part], preferred_element_type=jnp.float32
-                    )
-                    left[a, part] = both[:rows_dev] + both[rows_dev:]
+                both = jnp.dot(e_left[...], full[st][a], preferred_element_type=jnp.float32)
+                left[a] = both[:tall] + both[tall:]
 
         across.wait_recv()
 
@@ -419,31 +444,22 @@
         ahead = step_size if st == STAGES - 2 else 0.5 * step_size
 
         @pl.loop(0, n_aux, unroll=8)
-        def _(a, st=st, c=c, cut=cut, weight=weight, ahead=ahead):
+        def _(a, st=st, c=c, cut=cut, both_cut=both_cut, weight=weight, ahead=ahead):
             came = run[plan[2 * half + n_aux + a, 0]] + take[st][c][a].astype(jnp.float32)
-            prod_r = left[a, 0, cut, :] - right[a, 0]
-            prod_i = left[a, 1, cut, :] - right[a, 1]
-            rate = rate_ref[a]
-            base_r = real_ref[a, cut, :]
-            base_i = imag_ref[a, cut, :]
-            now_r = base_r if st == 0 else now[a, 0, cut, :]
-            now_i = base_i if st == 0 else now[a, 1, cut, :]
-            k_r = prod_i - rate * now_r + came[0]
-            k_i = came[1] - prod_r - rate * now_i
-            tot_r = (base_r if st == 0 else total[a, 0, cut, :]) + weight * k_r
-            tot_i = (base_i if st == 0 else total[a, 1, cut, :]) + weight * k_i
+            prod = left[a, both_cut, :] - right[a]
+            turn = jnp.concatenate([prod[rows:], -prod[:rows]], axis=0)
+            base = base_of(a, cut)
+            here = base if st == 0 else now[a, both_cut, :]
+            slope = turn - rate_ref[a] * here + came
+            sums = (base if st == 0 else total[a, both_cut, :]) + weight * slope
             if st == STAGES - 1:
-                outr_ref[a, cut, :] = tot_r
-                outi_ref[a, cut, :] = tot_i
+                outr_ref[a, cut, :] = sums[:rows]
+                outi_ref[a, cut, :] = sums[rows:]
             else:
-                total[a, 0, cut, :] = tot_r
-                total[a, 1, cut, :] = tot_i
-                next_r = base_r + ahead * k_r
-                next_i = base_i + ahead * k_i
-                now[a, 0, cut, :] = next_r
-                now[a, 1, cut, :] = next_i
-                place(st + 1, c, a, 0, next_r)
-                place(st + 1, c, a, 1, next_i)
+                total[a, both_cut, :] = sums
+                ahead_x = base + ahead * slope
+                now[a, both_cut, :] = ahead_x
+                place(st + 1, c, a, ahead_x)
 
         if st < STAGES - 1:
             share(st + 1, c)
@@ -479,11 +495,11 @@
 
     rows = rows_dev // CHUNKS
     bf16, f32 = jnp.bfloat16, jnp.float32
-    piece = pltpu.VMEM((n_aux, 2, rows, width), bf16)
+    piece = pltpu.VMEM((n_aux, 2 * rows, width), bf16)
     grid = (STAGES, CHUNKS)
     scratch = (
-        [pltpu.VMEM((lines * n_aux, 2, rows, width), bf16)] * (STAGES * CHUNKS)
-        + [pltpu.VMEM((n_aux, 2, row_devs * rows_dev, width), bf16)] * STAGES
+        [pltpu.VMEM((lines * n_aux, 2 * rows, width), bf16)] * (STAGES * CHUNKS)
+        + [pltpu.VMEM((n_aux, 2 * row_devs * rows_dev, width), bf16)] * STAGES
         + [piece] * (2 * STAGES * CHUNKS)
         + [
             pltpu.VMEM((n_aux, rows_dev, width), f32),
@@ -497,12 +513,12 @@
         ]
         + [pltpu.VMEM((8, lanes), jnp.int32)] * lines
         + [
-            pltpu.VMEM((half + 1, 2, rows, width), f32),
-            pltpu.VMEM((n_aux, 2, rows_dev, width), f32),
-            pltpu.VMEM((n_aux, 2, rows_dev, width), f32),
-            pltpu.VMEM((n_aux, 2, rows_dev, width), f32),
-            pltpu.VMEM((n_aux, 2, rows, width), f32),
-            pltpu.VMEM((2 * rows_dev, width), bf16),
+            pltpu.VMEM((half + 1, 2 * rows, width), f32),
+            pltpu.VMEM((n_aux, 2 * rows_dev, width), f32),
+            pltpu.VMEM((n_aux, 2 * rows_dev, width), f32),
+            pltpu.VMEM((n_aux, 2 * rows_dev, width), f32),
+            pltpu.VMEM((n_aux, 2 * rows, width), f32),
+            pltpu.VMEM((4 * rows_dev, 2 * width), bf16),
             pltpu.VMEM((width, 2 * width), bf16),
             dma(grid + (2, lines - 1)),
             dma(grid + (2, lines - 1)),
@@ -546,8 +562,8 @@
         slots = max(1, -(-n_aux * couplings.shape[2] // devices))
         terms_sent = (devices - 1) * slots
         states_sent = devices // 2 * n_aux
-        even = devices % 2 == 0 and devices > 2 and mesh.shape["row"] > 1
-        if even and states_sent < terms_sent and rows_dev % (16 * CHUNKS) == 0:
+        even = devices % 2 == 0 and devices > 4 and mesh.shape["row"] > 1
+        if even and states_sent < terms_sent and rows_dev % (8 * CHUNKS) == 0:
             return by_states(*args)
         return by_terms(*args)
 

time: 92 us -> 90.8 us (0.987)
  Pallas kernels: 87.2 us -> 86 us
    pallas_call x1, Pallas kernels: 87.2 us -> 86 us  [by_states(): pl.pallas_call(functools.partial(kernel, lines, row_devs, half, count, pe...]
where the time goes in v5:
time: 90.8 us; the launch traced here: 90.5 us
  Pallas kernels  86 us (95%)
  local copies, waits for them, and re-layouts  3.91 us (4%)
    pallas_call x1, Pallas kernels, by_states(): pl.pallas_call(functools.partial(kernel, lines, row_devs, half, count, pe...  86 us
    unnamed x4, local copies, waits for them, and re-layouts  2.42 us

profile of v5, /device:TPU:0, one launch (start us, length us, event | category | flops | bytes accessed | tf_op | source)
XLA Modules:
  0.0 90.5 jit_solution(995091616013194292)
XLA Ops:
  0.6 0.8 copy.10
  1.4 0.1 reshape.7
  1.5 0.6 pad.4.link_ref
  2.1 86.0 %shard_map.86 = (f32[16,32,128]{2,1,0:T(8,128)}, f32[16,32,128]{2,1,0:T(8,128)}) custom-call(f32[16]{0:T(128)} %rate_ref.1, f32[2,128]{1,0:T(2,128)} %coef_ref.1, f32[16,32,128]{2,1,0:T(8,128)} %real_in.1, f32[16,32,128]{2,1,0:T(8,128)} %imag_in.1, f32[128,128]{1,0:T(8,128)} %ham_ref.1, f32[128,128]{1,0:T(8,128)} %mode_ref.1, s32[8,128]{1,0:T(8,128)} %pad.4.link_ref), custom_call_target="tpu_custom_call" | custom-call | tf_op jit(solution)/shard_map/pallas_call | solution.py:535
  88.1 0.0 copy-start
  88.1 1.7 %copy.13 = f32[16,32,128]{2,1,0:T(8,128)} copy(f32[16,32,128]{2,1,0:T(8,128)} %get-tuple-element.4) | data formatting | bytes 524288
  89.8 0.0 copy-done
  89.8 0.7 copy.14
Async XLA Ops:
  88.1 1.7 %copy-start = (f32[16,32,128]{2,1,0:T(8,128)S(1)}, f32[16,32,128]{2,1,0:T(8,128)}, u32[]{:S(2)}) copy-start(f32[16,32,128]{2,1,0:T(8,128)} %get-tuple-element.5) | copy-start | bytes 786436

commit v6 on v5

--- a/solution.py
+++ b/solution.py
@@ -12,6 +12,8 @@
 MESH = pl.DeviceIdType.MESH
 CHUNKS = 4
 STAGES = 4
+GROUPS = 4
+LINES = 4
 
 
 def as_sent(x):
@@ -145,10 +147,12 @@
     full = [scratch.pop(0) for _ in range(STAGES)]
     give = [[scratch.pop(0) for _ in range(CHUNKS)] for _ in range(STAGES)]
     take = [[scratch.pop(0) for _ in range(CHUNKS)] for _ in range(STAGES)]
+    fold = [[scratch.pop(0) for _ in range(CHUNKS)] for _ in range(STAGES)]
+    land = [[scratch.pop(0) for _ in range(CHUNKS)] for _ in range(STAGES)]
     real_ref, imag_ref, energy_ref, facr_ref, faci_ref, turned, lists, plan = scratch[:8]
     links = scratch[8 : 8 + lines]
-    run, now, total, left, right, e_left, e_right = scratch[8 + lines : 15 + lines]
-    zs, zr, rs, rr, ys, yr, ls, lr, ins = scratch[15 + lines :]
+    run, run_own, came, now, total, left, right, e_left, e_right = scratch[8 + lines : 17 + lines]
+    zs, zr, rs, rr, ys, yr, fs, fr, ls, lr, ins = scratch[17 + lines :]
 
     fetched = [
         pltpu.make_async_copy(real_in, real_ref, ins.at[0]),
@@ -164,6 +168,10 @@
     beside = aux + 1 - 2 * side
     row_peers = [lax.rem(row + k, row_devs) for k in range(1, row_devs)]
     last_line = lines - 1
+    inner = (line > 0) & (line < last_line)
+    at_end = (line == 0) | (line == last_line)
+    end_line = jnp.where(line < lines // 2, 0, last_line)
+    outward = aux + 2 * (end_line - line)
 
     barrier = pltpu.get_barrier_semaphore()
 
@@ -189,6 +197,26 @@
         return c
 
     row_copies = {}
+
+    def across_copy(st, c):
+        return pltpu.make_async_remote_copy(
+            src_ref=give[st][c],
+            dst_ref=take[st][c],
+            send_sem=ys.at[st, c],
+            recv_sem=yr.at[st, c],
+            device_id=(beside, row),
+            device_id_type=MESH,
+        )
+
+    def fold_copy(st, c):
+        return pltpu.make_async_remote_copy(
+            src_ref=fold[st][c],
+            dst_ref=land[st][c],
+            send_sem=fs.at[st, c],
+            recv_sem=fr.at[st, c],
+            device_id=(outward, row),
+            device_id_type=MESH,
+        )
 
     def own_rows(c):
         return pl.ds(pl.multiple_of((row * CHUNKS + c) * pair, pair), pair)
@@ -209,11 +237,13 @@
 
     def hop_sends(hop, way):
         if way == 0:
-            return (line >= hop - 1) & (line < last_line)
-        return (line + hop - 1 <= last_line) & (line > 0)
+            return (line >= hop - 1) & (line < last_line - 1)
+        return (line + hop - 1 <= last_line) & (line > 1)
 
     def hop_gets(hop, way):
-        return line >= hop if way == 0 else line + hop <= last_line
+        if way == 0:
+            return (line >= hop) & (line < last_line)
+        return (line + hop <= last_line) & (line > 0)
 
     def hop_send(st, c, hop):
         for way in range(2):
@@ -233,7 +263,7 @@
 
     def hop_relay(st, c, hop):
         hop_get(st, c, hop)
-        if hop < lines - 1:
+        if hop < lines - 2:
             hop_send(st, c, hop + 1)
 
     def share(st, c):
@@ -307,6 +337,7 @@
         )
         e_left[k * tall : (k + 1) * tall] = jnp.where(same_part, spread, 0.0).astype(jnp.bfloat16)
     run[0] = jnp.zeros(run.shape[1:], jnp.float32)
+    run_own[0] = jnp.zeros(run.shape[1:], jnp.float32)
 
     turned[...] = mode_ref[...].T
     links[0][...] = link_ref[...]
@@ -323,8 +354,11 @@
         from_line = lax.rem(line - k + lines, lines)
         target = links[k][0:1, :]
         dest = target // n_aux
-        chosen = (dest // 2 == line) & (lane < count)
-        group = jnp.where(lax.rem(dest, 2) == side, 1, 0)
+        goes_to = dest // 2
+        own_line = jnp.where(inner | (from_line == line), line, -1)
+        fold_line = jnp.where(inner & (from_line != end_line), end_line, -1)
+        chosen = ((goes_to == own_line) | (goes_to == fold_line)) & (lane < count)
+        group = jnp.where(lax.rem(dest, 2) == side, 1, 0) + jnp.where(goes_to == line, 0, 2)
         key = group * n_aux + lax.rem(target, n_aux)
         place_in = from_line * lanes + lane
         key = jnp.where(chosen, key * (lines * lanes) + place_in, far)
@@ -341,28 +375,36 @@
     rank = jnp.sum(jnp.where(before, 1, 0), axis=0, keepdims=True)
     again = jnp.sum(jnp.where(before & (column // span == key // span), 1, 0), axis=0, keepdims=True)
     second = n_aux * span
-    first_count = jnp.sum(jnp.where(key < second, 1, 0), axis=1, keepdims=True)
-    ranked = jnp.where(key < second, rank, rank - first_count)
-    slot = jnp.where(key < second, ranked, ranked + half)
+    which = lax.broadcasted_iota(i32, (GROUPS * n_aux, 1), 0)
+    ranked, skipped = rank, jnp.zeros_like(which)
+    for g in range(GROUPS - 1):
+        inside = (key >= g * second) & (key < (g + 1) * second)
+        size = jnp.sum(jnp.where(inside, 1, 0), axis=1, keepdims=True)
+        ranked = ranked - jnp.where(key >= (g + 1) * second, size, 0)
+        skipped = skipped + jnp.where(which >= (g + 1) * n_aux, size, 0)
+    slot = key // second * half + ranked
     slot = jnp.where(chosen & (ranked < half), slot, -1)
-    pick = lax.broadcasted_iota(i32, (2 * half, span), 0) == slot
+    pick = lax.broadcasted_iota(i32, (GROUPS * half, span), 0) == slot
 
     def picked(values):
         return jnp.sum(jnp.where(pick, values, 0), axis=1, keepdims=True)
 
-    at = lax.broadcasted_iota(i32, (2 * half, 128), 1)
-    table = jnp.where(at == 0, picked(jnp.concatenate(source_row, axis=1)), 0)
+    at = lax.broadcasted_iota(i32, (GROUPS * half, 128), 1)
+    filled = picked(jnp.ones_like(key))
+    source = picked(jnp.concatenate(source_row, axis=1)) + (1 - filled) * line * n_aux
+    table = jnp.where(at == 0, source, 0)
     table = jnp.where(at == 1, picked(jnp.concatenate(modes_row, axis=1)), table)
     table = jnp.where(at == 2, picked(jnp.concatenate(weights_row, axis=1)), table)
     table = jnp.where(at == 3, picked(jnp.where(again > 0, 1, 0)), table)
-    table = jnp.where(at == 4, picked(jnp.ones_like(key)), table)
-    lists[: 2 * half] = table
-    wanted = lax.broadcasted_iota(i32, (2 * n_aux, span), 0)
+    table = jnp.where(at == 4, filled, table)
+    lists[: GROUPS * half] = table
+    wanted = lax.broadcasted_iota(i32, (GROUPS * n_aux, span), 0)
     upto = jnp.sum(jnp.where(key < (wanted + 1) * span, 1, 0), axis=1, keepdims=True)
     here = jnp.sum(jnp.where(key // span == wanted, 1, 0), axis=1, keepdims=True)
-    which = lax.broadcasted_iota(i32, (2 * n_aux, 1), 0)
-    upto = jnp.minimum(jnp.where(which < n_aux, upto, upto - first_count), half)
-    lists[2 * half :] = jnp.broadcast_to(jnp.where(here > 0, upto, 0), (2 * n_aux, 128))
+    upto = jnp.minimum(upto - skipped, half)
+    lists[GROUPS * half :] = jnp.broadcast_to(
+        jnp.where(here > 0, upto, 0), (GROUPS * n_aux, 128)
+    )
     planned = pltpu.make_async_copy(lists, plan, ins.at[2])
     planned.start()
     steps = [(st, c) for st in range(STAGES) for c in range(CHUNKS)]
@@ -372,7 +414,7 @@
 
     mode_lane = lax.broadcasted_iota(i32, (rows_dev, mode_ref.shape[0]), 1)
 
-    @pl.loop(0, 2 * half, unroll=8)
+    @pl.loop(0, GROUPS * half, unroll=8)
     def _(e):
         m = plan[e, 1]
         w = plan[e, 2]
@@ -385,7 +427,7 @@
         facr_ref[e] = plus * (down + across)
         faci_ref[e] = -minus * (down - across)
 
-    def gather_sum(st, c, group):
+    def gather_sum(st, c, group, run):
         cut = slice(c * rows, (c + 1) * rows)
 
         def body(e, acc):
@@ -406,28 +448,74 @@
         zero = jnp.zeros((rows, width), jnp.float32)
         lax.fori_loop(0, half, body, (zero, zero), unroll=12)
 
-    hop_relay(*steps[0], 2)
+    def last_of(group, a):
+        return plan[GROUPS * half + group * n_aux + a, 0]
+
+    def fold_out(st, c):
+        hop_get(st, c, 2)
+
+        @pl.when(inner)
+        def _():
+            for g in range(2):
+                gather_sum(st, c, 2 + g, run)
+
+                @pl.loop(0, n_aux, unroll=8)
+                def _(a):
+                    fold[st][c][g * n_aux + a] = run[last_of(2 + g, a)].astype(jnp.bfloat16)
+
+            fold_copy(st, c).start()
+
+    fold_out(*steps[0])
     for n, (st, c) in enumerate(steps):
         cut = slice(c * rows, (c + 1) * rows)
         both_cut = slice(c * pair, (c + 1) * pair)
-        for hop in range(3, lines):
-            hop_relay(st, c, hop)
-        gather_sum(st, c, 0)
-
-        @pl.loop(0, n_aux, unroll=8)
-        def _(a, st=st, c=c):
-            give[st][c][a] = run[plan[2 * half + a, 0]].astype(jnp.bfloat16)
-
-        across = send(give[st][c], take[st][c], ys.at[st, c], yr.at[st, c], (beside, row))
-        if n + 1 < len(steps):
-            hop_relay(*steps[n + 1], 2)
+        gather_sum(st, c, 0, run)
+
+        @pl.when(inner)
+        def _(st=st, c=c):
+            @pl.loop(0, n_aux, unroll=8)
+            def _(a):
+                give[st][c][a] = run[last_of(0, a)].astype(jnp.bfloat16)
+
+            across_copy(st, c).start()
+
+        @pl.when(at_end)
+        def _():
+            @pl.loop(0, n_aux, unroll=8)
+            def _(a):
+                came[a] = run[last_of(0, a)]
+
         if n + 2 < len(steps):
             hop_relay(*steps[n + 2], 1)
+        gather_sum(st, c, 1, run_own)
+        if n + 1 < len(steps):
+            fold_out(*steps[n + 1])
+
+        @pl.when(at_end)
+        def _(st=st, c=c):
+            fold_copy(st, c).wait_recv()
+
+            @pl.loop(0, n_aux, unroll=8)
+            def _(a):
+                both_sums = came[a] + land[st][c][a].astype(jnp.float32)
+                give[st][c][a] = both_sums.astype(jnp.bfloat16)
+
+            across_copy(st, c).start()
+
+            @pl.loop(0, n_aux, unroll=8)
+            def _(a):
+                came[a] = run_own[last_of(1, a)] + land[st][c][n_aux + a].astype(jnp.float32)
+
+        @pl.when(inner)
+        def _():
+            @pl.loop(0, n_aux, unroll=8)
+            def _(a):
+                came[a] = run_own[last_of(1, a)]
+
         own = pl.ds(pl.multiple_of(line * n_aux, n_aux), n_aux)
         flat = held[st][c][own].reshape(n_aux * pair, width)
         both = jnp.dot(flat, e_right[...], preferred_element_type=jnp.float32)
         right[...] = (both[:, :width] + both[:, width:]).reshape(n_aux, pair, width)
-        gather_sum(st, c, 1)
         if c == 0:
             for cc in range(CHUNKS):
                 for d in row_copies[st, cc]:
@@ -438,19 +526,19 @@
                 both = jnp.dot(e_left[...], full[st][a], preferred_element_type=jnp.float32)
                 left[a] = both[:tall] + both[tall:]
 
-        across.wait_recv()
+        across_copy(st, c).wait_recv()
 
         weight = step_size / 6.0 * (1.0 if st in (0, STAGES - 1) else 2.0)
         ahead = step_size if st == STAGES - 2 else 0.5 * step_size
 
         @pl.loop(0, n_aux, unroll=8)
         def _(a, st=st, c=c, cut=cut, both_cut=both_cut, weight=weight, ahead=ahead):
-            came = run[plan[2 * half + n_aux + a, 0]] + take[st][c][a].astype(jnp.float32)
+            arrived = came[a] + take[st][c][a].astype(jnp.float32)
             prod = left[a, both_cut, :] - right[a]
             turn = jnp.concatenate([prod[rows:], -prod[:rows]], axis=0)
             base = base_of(a, cut)
             here = base if st == 0 else now[a, both_cut, :]
-            slope = turn - rate_ref[a] * here + came
+            slope = turn - rate_ref[a] * here + arrived
             sums = (base if st == 0 else total[a, both_cut, :]) + weight * slope
             if st == STAGES - 1:
                 outr_ref[a, cut, :] = sums[:rows]
@@ -467,7 +555,13 @@
     for d in copies:
         d.wait_send()
     for st, c in steps:
-        for hop in range(1, lines):
+        across_copy(st, c).wait_send()
+
+        @pl.when(inner)
+        def _(st=st, c=c):
+            fold_copy(st, c).wait_send()
+
+        for hop in range(1, lines - 1):
             for way in range(2):
 
                 @pl.when(hop_sends(hop, way))
@@ -501,29 +595,34 @@
         [pltpu.VMEM((lines * n_aux, 2 * rows, width), bf16)] * (STAGES * CHUNKS)
         + [pltpu.VMEM((n_aux, 2 * row_devs * rows_dev, width), bf16)] * STAGES
         + [piece] * (2 * STAGES * CHUNKS)
+        + [pltpu.VMEM((2 * n_aux, 2 * rows, width), bf16)] * (2 * STAGES * CHUNKS)
         + [
             pltpu.VMEM((n_aux, rows_dev, width), f32),
             pltpu.VMEM((n_aux, rows_dev, width), f32),
             pltpu.VMEM((width, width), f32),
-            pltpu.VMEM((2 * half, rows_dev, width), f32),
-            pltpu.VMEM((2 * half, rows_dev, width), f32),
+            pltpu.VMEM((GROUPS * half, rows_dev, width), f32),
+            pltpu.VMEM((GROUPS * half, rows_dev, width), f32),
             pltpu.VMEM((width, mode_vector.shape[0]), f32),
-            pltpu.VMEM((2 * half + 2 * n_aux, 128), jnp.int32),
-            pltpu.SMEM((2 * half + 2 * n_aux, 128), jnp.int32),
+            pltpu.VMEM((GROUPS * (half + n_aux), 128), jnp.int32),
+            pltpu.SMEM((GROUPS * (half + n_aux), 128), jnp.int32),
         ]
         + [pltpu.VMEM((8, lanes), jnp.int32)] * lines
         + [
             pltpu.VMEM((half + 1, 2 * rows, width), f32),
+            pltpu.VMEM((half + 1, 2 * rows, width), f32),
+            pltpu.VMEM((n_aux, 2 * rows, width), f32),
             pltpu.VMEM((n_aux, 2 * rows_dev, width), f32),
             pltpu.VMEM((n_aux, 2 * rows_dev, width), f32),
             pltpu.VMEM((n_aux, 2 * rows_dev, width), f32),
             pltpu.VMEM((n_aux, 2 * rows, width), f32),
             pltpu.VMEM((4 * rows_dev, 2 * width), bf16),
             pltpu.VMEM((width, 2 * width), bf16),
-            dma(grid + (2, lines - 1)),
-            dma(grid + (2, lines - 1)),
+            dma(grid + (2, lines - 2)),
+            dma(grid + (2, lines - 2)),
             dma(grid + (row_devs - 1,)),
             dma(grid + (row_devs - 1,)),
+            dma(grid),
+            dma(grid),
             dma(grid),
             dma(grid),
             dma((lines - 1,)),
@@ -562,7 +661,7 @@
         slots = max(1, -(-n_aux * couplings.shape[2] // devices))
         terms_sent = (devices - 1) * slots
         states_sent = devices // 2 * n_aux
-        even = devices % 2 == 0 and devices > 4 and mesh.shape["row"] > 1
+        even = devices == 2 * LINES and mesh.shape["row"] > 1
         if even and states_sent < terms_sent and rows_dev % (8 * CHUNKS) == 0:
             return by_states(*args)
         return by_terms(*args)

time: 90.8 us -> 94.6 us (1.042)
  Pallas kernels: 86 us -> 89.8 us
    pallas_call x1, Pallas kernels: 86 us -> 89.8 us  [by_states(): pl.pallas_call(functools.partial(kernel, lines, row_devs, half, count, pe...]
where the time goes in v6:
time: 94.6 us; the launch traced here: 94.4 us
  Pallas kernels  89.8 us (95%)
  local copies, waits for them, and re-layouts  3.91 us (4%)
    pallas_call x1, Pallas kernels, by_states(): pl.pallas_call(functools.partial(kernel, lines, row_devs, half, count, pe...  89.8 us
    unnamed x4, local copies, waits for them, and re-layouts  2.42 us

profile of v6, /device:TPU:0, one launch (start us, length us, event | category | flops | bytes accessed | tf_op | source)
XLA Modules:
  0.0 94.4 jit_solution(9463869686915607419)
XLA Ops:
  0.6 0.8 copy.10
  1.4 0.1 reshape.7
  1.5 0.6 pad.4.link_ref
  2.1 89.8 %shard_map.86 = (f32[16,32,128]{2,1,0:T(8,128)}, f32[16,32,128]{2,1,0:T(8,128)}) custom-call(f32[16]{0:T(128)} %rate_ref.1, f32[2,128]{1,0:T(2,128)} %coef_ref.1, f32[16,32,128]{2,1,0:T(8,128)} %real_in.1, f32[16,32,128]{2,1,0:T(8,128)} %imag_in.1, f32[128,128]{1,0:T(8,128)} %ham_ref.1, f32[128,128]{1,0:T(8,128)} %mode_ref.1, s32[8,128]{1,0:T(8,128)} %pad.4.link_ref), custom_call_target="tpu_custom_call" | custom-call | tf_op jit(solution)/shard_map/pallas_call | solution.py:634
  92.0 0.0 copy-start
  92.0 1.7 %copy.13 = f32[16,32,128]{2,1,0:T(8,128)} copy(f32[16,32,128]{2,1,0:T(8,128)} %get-tuple-element.4) | data formatting | bytes 524288
  93.7 0.0 copy-done
  93.7 0.7 copy.14
Async XLA Ops:
  92.0 1.7 %copy-start = (f32[16,32,128]{2,1,0:T(8,128)S(1)}, f32[16,32,128]{2,1,0:T(8,128)}, u32[]{:S(2)}) copy-start(f32[16,32,128]{2,1,0:T(8,128)} %get-tuple-element.5) | copy-start | bytes 786436

commit v7 on v6

--- a/solution.py
+++ b/solution.py
@@ -427,7 +427,7 @@
         facr_ref[e] = plus * (down + across)
         faci_ref[e] = -minus * (down - across)
 
-    def gather_sum(st, c, group, run):
+    def gather_sum(st, c, group, run, entries):
         cut = slice(c * rows, (c + 1) * rows)
 
         def body(e, acc):
@@ -446,7 +446,7 @@
             return ar, ai
 
         zero = jnp.zeros((rows, width), jnp.float32)
-        lax.fori_loop(0, half, body, (zero, zero), unroll=12)
+        lax.fori_loop(0, entries, body, (zero, zero), unroll=12)
 
     def last_of(group, a):
         return plan[GROUPS * half + group * n_aux + a, 0]
@@ -457,7 +457,7 @@
         @pl.when(inner)
         def _():
             for g in range(2):
-                gather_sum(st, c, 2 + g, run)
+                gather_sum(st, c, 2 + g, run, half - half // lines)
 
                 @pl.loop(0, n_aux, unroll=8)
                 def _(a):
@@ -465,14 +465,14 @@
 
             fold_copy(st, c).start()
 
-    fold_out(*steps[0])
-    for n, (st, c) in enumerate(steps):
-        cut = slice(c * rows, (c + 1) * rows)
-        both_cut = slice(c * pair, (c + 1) * pair)
-        gather_sum(st, c, 0, run)
+    def sums_out(n):
+        st, c = steps[n]
+        turn = n % 2
+        fold_out(st, c)
+        gather_sum(st, c, 0, run, half)
 
         @pl.when(inner)
-        def _(st=st, c=c):
+        def _():
             @pl.loop(0, n_aux, unroll=8)
             def _(a):
                 give[st][c][a] = run[last_of(0, a)].astype(jnp.bfloat16)
@@ -483,39 +483,43 @@
         def _():
             @pl.loop(0, n_aux, unroll=8)
             def _(a):
-                came[a] = run[last_of(0, a)]
-
-        if n + 2 < len(steps):
-            hop_relay(*steps[n + 2], 1)
-        gather_sum(st, c, 1, run_own)
-        if n + 1 < len(steps):
-            fold_out(*steps[n + 1])
-
-        @pl.when(at_end)
-        def _(st=st, c=c):
-            fold_copy(st, c).wait_recv()
-
-            @pl.loop(0, n_aux, unroll=8)
-            def _(a):
-                both_sums = came[a] + land[st][c][a].astype(jnp.float32)
-                give[st][c][a] = both_sums.astype(jnp.bfloat16)
-
-            across_copy(st, c).start()
-
-            @pl.loop(0, n_aux, unroll=8)
-            def _(a):
-                came[a] = run_own[last_of(1, a)] + land[st][c][n_aux + a].astype(jnp.float32)
-
-        @pl.when(inner)
-        def _():
-            @pl.loop(0, n_aux, unroll=8)
-            def _(a):
-                came[a] = run_own[last_of(1, a)]
+                came[2 + turn, a] = run[last_of(0, a)]
+
+        gather_sum(st, c, 1, run_own, half)
+
+        @pl.loop(0, n_aux, unroll=8)
+        def _(a):
+            came[turn, a] = run_own[last_of(1, a)]
 
         own = pl.ds(pl.multiple_of(line * n_aux, n_aux), n_aux)
         flat = held[st][c][own].reshape(n_aux * pair, width)
         both = jnp.dot(flat, e_right[...], preferred_element_type=jnp.float32)
-        right[...] = (both[:, :width] + both[:, width:]).reshape(n_aux, pair, width)
+        right[turn] = (both[:, :width] + both[:, width:]).reshape(n_aux, pair, width)
+
+    def end_out(n):
+        st, c = steps[n]
+        turn = n % 2
+
+        @pl.when(at_end)
+        def _():
+            fold_copy(st, c).wait_recv()
+
+            @pl.loop(0, n_aux, unroll=8)
+            def _(a):
+                both_sums = came[2 + turn, a] + land[st][c][a].astype(jnp.float32)
+                give[st][c][a] = both_sums.astype(jnp.bfloat16)
+
+            across_copy(st, c).start()
+
+            @pl.loop(0, n_aux, unroll=8)
+            def _(a):
+                came[turn, a] += land[st][c][n_aux + a].astype(jnp.float32)
+
+    def finish(n):
+        st, c = steps[n]
+        order = n % 2
+        cut = slice(c * rows, (c + 1) * rows)
+        both_cut = slice(c * pair, (c + 1) * pair)
         if c == 0:
             for cc in range(CHUNKS):
                 for d in row_copies[st, cc]:
@@ -533,8 +537,8 @@
 
         @pl.loop(0, n_aux, unroll=8)
         def _(a, st=st, c=c, cut=cut, both_cut=both_cut, weight=weight, ahead=ahead):
-            arrived = came[a] + take[st][c][a].astype(jnp.float32)
-            prod = left[a, both_cut, :] - right[a]
+            arrived = came[order, a] + take[st][c][a].astype(jnp.float32)
+            prod = left[a, both_cut, :] - right[order, a]
             turn = jnp.concatenate([prod[rows:], -prod[:rows]], axis=0)
             base = base_of(a, cut)
             here = base if st == 0 else now[a, both_cut, :]
@@ -551,6 +555,16 @@
 
         if st < STAGES - 1:
             share(st + 1, c)
+
+    for n in range(len(steps) + 1):
+        if n < len(steps):
+            sums_out(n)
+        if n > 0:
+            end_out(n - 1)
+        if n + 2 < len(steps):
+            hop_relay(*steps[n + 2], 1)
+        if n > 0:
+            finish(n - 1)
 
     for d in copies:
         d.wait_send()
@@ -610,11 +624,11 @@
         + [
             pltpu.VMEM((half + 1, 2 * rows, width), f32),
             pltpu.VMEM((half + 1, 2 * rows, width), f32),
-            pltpu.VMEM((n_aux, 2 * rows, width), f32),
+            pltpu.VMEM((4, n_aux, 2 * rows, width), f32),
             pltpu.VMEM((n_aux, 2 * rows_dev, width), f32),
             pltpu.VMEM((n_aux, 2 * rows_dev, width), f32),
             pltpu.VMEM((n_aux, 2 * rows_dev, width), f32),
-            pltpu.VMEM((n_aux, 2 * rows, width), f32),
+            pltpu.VMEM((2, n_aux, 2 * rows, width), f32),
             pltpu.VMEM((4 * rows_dev, 2 * width), bf16),
             pltpu.VMEM((width, 2 * width), bf16),
             dma(grid + (2, lines - 2)),

time: 94.6 us -> 97 us (1.025)
  Pallas kernels: 89.8 us -> 92.2 us
    pallas_call x1, Pallas kernels: 89.8 us -> 92.2 us  [by_states(): pl.pallas_call(functools.partial(kernel, lines, row_devs, half, count, pe...]
where the time goes in v7:
time: 97 us; the launch traced here: 96.8 us
  Pallas kernels  92.2 us (95%)
  local copies, waits for them, and re-layouts  3.91 us (4%)
    pallas_call x1, Pallas kernels, by_states(): pl.pallas_call(functools.partial(kernel, lines, row_devs, half, count, pe...  92.2 us
    unnamed x4, local copies, waits for them, and re-layouts  2.42 us

profile of v7, /device:TPU:0, one launch (start us, length us, event | category | flops | bytes accessed | tf_op | source)
XLA Modules:
  0.0 96.8 jit_solution(13082691384291970954)
XLA Ops:
  0.6 0.8 copy.10
  1.4 0.1 reshape.7
  1.5 0.6 pad.4.link_ref
  2.1 92.2 %shard_map.86 = (f32[16,32,128]{2,1,0:T(8,128)}, f32[16,32,128]{2,1,0:T(8,128)}) custom-call(f32[16]{0:T(128)} %rate_ref.1, f32[2,128]{1,0:T(2,128)} %coef_ref.1, f32[16,32,128]{2,1,0:T(8,128)} %real_in.1, f32[16,32,128]{2,1,0:T(8,128)} %imag_in.1, f32[128,128]{1,0:T(8,128)} %ham_ref.1, f32[128,128]{1,0:T(8,128)} %mode_ref.1, s32[8,128]{1,0:T(8,128)} %pad.4.link_ref), custom_call_target="tpu_custom_call" | custom-call | tf_op jit(solution)/shard_map/pallas_call | solution.py:648
  94.3 0.0 copy-start
  94.3 1.7 %copy.13 = f32[16,32,128]{2,1,0:T(8,128)} copy(f32[16,32,128]{2,1,0:T(8,128)} %get-tuple-element.4) | data formatting | bytes 524288
  96.1 0.0 copy-done
  96.1 0.7 copy.14
Async XLA Ops:
  94.3 1.7 %copy-start = (f32[16,32,128]{2,1,0:T(8,128)S(1)}, f32[16,32,128]{2,1,0:T(8,128)}, u32[]{:S(2)}) copy-start(f32[16,32,128]{2,1,0:T(8,128)} %get-tuple-element.5) | copy-start | bytes 786436

commit v8 on v5

--- a/solution.py
+++ b/solution.py
@@ -147,8 +147,8 @@
     take = [[scratch.pop(0) for _ in range(CHUNKS)] for _ in range(STAGES)]
     real_ref, imag_ref, energy_ref, facr_ref, faci_ref, turned, lists, plan = scratch[:8]
     links = scratch[8 : 8 + lines]
-    run, now, total, left, right, e_left, e_right = scratch[8 + lines : 15 + lines]
-    zs, zr, rs, rr, ys, yr, ls, lr, ins = scratch[15 + lines :]
+    run, came, now, total, left, right, e_left, e_right = scratch[8 + lines : 16 + lines]
+    zs, zr, rs, rr, ys, yr, ls, lr, ins = scratch[16 + lines :]
 
     fetched = [
         pltpu.make_async_copy(real_in, real_ref, ins.at[0]),
@@ -406,28 +406,40 @@
         zero = jnp.zeros((rows, width), jnp.float32)
         lax.fori_loop(0, half, body, (zero, zero), unroll=12)
 
-    hop_relay(*steps[0], 2)
-    for n, (st, c) in enumerate(steps):
-        cut = slice(c * rows, (c + 1) * rows)
-        both_cut = slice(c * pair, (c + 1) * pair)
+    across = {}
+
+    def sums_out(n):
+        st, c = steps[n]
+        turn = n % 2
         for hop in range(3, lines):
             hop_relay(st, c, hop)
         gather_sum(st, c, 0)
 
         @pl.loop(0, n_aux, unroll=8)
-        def _(a, st=st, c=c):
+        def _(a):
             give[st][c][a] = run[plan[2 * half + a, 0]].astype(jnp.bfloat16)
 
-        across = send(give[st][c], take[st][c], ys.at[st, c], yr.at[st, c], (beside, row))
+        across[n] = send(give[st][c], take[st][c], ys.at[st, c], yr.at[st, c], (beside, row))
         if n + 1 < len(steps):
             hop_relay(*steps[n + 1], 2)
-        if n + 2 < len(steps):
-            hop_relay(*steps[n + 2], 1)
+        gather_sum(st, c, 1)
+
+        @pl.loop(0, n_aux, unroll=8)
+        def _(a):
+            came[turn, a] = run[plan[2 * half + n_aux + a, 0]]
+
         own = pl.ds(pl.multiple_of(line * n_aux, n_aux), n_aux)
         flat = held[st][c][own].reshape(n_aux * pair, width)
         both = jnp.dot(flat, e_right[...], preferred_element_type=jnp.float32)
-        right[...] = (both[:, :width] + both[:, width:]).reshape(n_aux, pair, width)
-        gather_sum(st, c, 1)
+        right[turn] = (both[:, :width] + both[:, width:]).reshape(n_aux, pair, width)
+        if n + 2 < len(steps):
+            hop_relay(*steps[n + 2], 1)
+
+    def finish(n):
+        st, c = steps[n]
+        order = n % 2
+        cut = slice(c * rows, (c + 1) * rows)
+        both_cut = slice(c * pair, (c + 1) * pair)
         if c == 0:
             for cc in range(CHUNKS):
                 for d in row_copies[st, cc]:
@@ -438,19 +450,19 @@
                 both = jnp.dot(e_left[...], full[st][a], preferred_element_type=jnp.float32)
                 left[a] = both[:tall] + both[tall:]
 
-        across.wait_recv()
+        across[n].wait_recv()
 
         weight = step_size / 6.0 * (1.0 if st in (0, STAGES - 1) else 2.0)
         ahead = step_size if st == STAGES - 2 else 0.5 * step_size
 
         @pl.loop(0, n_aux, unroll=8)
         def _(a, st=st, c=c, cut=cut, both_cut=both_cut, weight=weight, ahead=ahead):
-            came = run[plan[2 * half + n_aux + a, 0]] + take[st][c][a].astype(jnp.float32)
-            prod = left[a, both_cut, :] - right[a]
+            arrived = came[order, a] + take[st][c][a].astype(jnp.float32)
+            prod = left[a, both_cut, :] - right[order, a]
             turn = jnp.concatenate([prod[rows:], -prod[:rows]], axis=0)
             base = base_of(a, cut)
             here = base if st == 0 else now[a, both_cut, :]
-            slope = turn - rate_ref[a] * here + came
+            slope = turn - rate_ref[a] * here + arrived
             sums = (base if st == 0 else total[a, both_cut, :]) + weight * slope
             if st == STAGES - 1:
                 outr_ref[a, cut, :] = sums[:rows]
@@ -463,6 +475,13 @@
 
         if st < STAGES - 1:
             share(st + 1, c)
+
+    hop_relay(*steps[0], 2)
+    for n in range(len(steps) + 1):
+        if n < len(steps):
+            sums_out(n)
+        if n > 0:
+            finish(n - 1)
 
     for d in copies:
         d.wait_send()
@@ -514,10 +533,11 @@
         + [pltpu.VMEM((8, lanes), jnp.int32)] * lines
         + [
             pltpu.VMEM((half + 1, 2 * rows, width), f32),
+            pltpu.VMEM((2, n_aux, 2 * rows, width), f32),
             pltpu.VMEM((n_aux, 2 * rows_dev, width), f32),
             pltpu.VMEM((n_aux, 2 * rows_dev, width), f32),
             pltpu.VMEM((n_aux, 2 * rows_dev, width), f32),
-            pltpu.VMEM((n_aux, 2 * rows, width), f32),
+            pltpu.VMEM((2, n_aux, 2 * rows, width), f32),
             pltpu.VMEM((4 * rows_dev, 2 * width), bf16),
             pltpu.VMEM((width, 2 * width), bf16),
             dma(grid + (2, lines - 1)),

time: 90.8 us -> 97 us (1.068)
  Pallas kernels: 86 us -> 92.2 us
    pallas_call x1, Pallas kernels: 86 us -> 92.2 us  [by_states(): pl.pallas_call(functools.partial(kernel, lines, row_devs, half, count, pe...]
where the time goes in v8:
time: 97 us; the launch traced here: 96.7 us
  Pallas kernels  92.2 us (95%)
  local copies, waits for them, and re-layouts  3.91 us (4%)
    pallas_call x1, Pallas kernels, by_states(): pl.pallas_call(functools.partial(kernel, lines, row_devs, half, count, pe...  92.2 us
    unnamed x4, local copies, waits for them, and re-layouts  2.42 us

profile of v8, /device:TPU:0, one launch (start us, length us, event | category | flops | bytes accessed | tf_op | source)
XLA Modules:
  0.0 96.7 jit_solution(16910284913368882199)
XLA Ops:
  0.6 0.8 copy.10
  1.4 0.1 reshape.7
  1.5 0.6 pad.4.link_ref
  2.1 92.2 %shard_map.86 = (f32[16,32,128]{2,1,0:T(8,128)}, f32[16,32,128]{2,1,0:T(8,128)}) custom-call(f32[16]{0:T(128)} %rate_ref.1, f32[2,128]{1,0:T(2,128)} %coef_ref.1, f32[16,32,128]{2,1,0:T(8,128)} %real_in.1, f32[16,32,128]{2,1,0:T(8,128)} %imag_in.1, f32[128,128]{1,0:T(8,128)} %ham_ref.1, f32[128,128]{1,0:T(8,128)} %mode_ref.1, s32[8,128]{1,0:T(8,128)} %pad.4.link_ref), custom_call_target="tpu_custom_call" | custom-call | tf_op jit(solution)/shard_map/pallas_call | solution.py:555
  94.3 0.0 copy-start
  94.3 1.7 %copy.13 = f32[16,32,128]{2,1,0:T(8,128)} copy(f32[16,32,128]{2,1,0:T(8,128)} %get-tuple-element.4) | data formatting | bytes 524288
  96.0 0.0 copy-done
  96.0 0.7 copy.14
Async XLA Ops:
  94.3 1.7 %copy-start = (f32[16,32,128]{2,1,0:T(8,128)S(1)}, f32[16,32,128]{2,1,0:T(8,128)}, u32[]{:S(2)}) copy-start(f32[16,32,128]{2,1,0:T(8,128)} %get-tuple-element.5) | copy-start | bytes 786436

commit v9 on v5

--- a/solution.py
+++ b/solution.py
@@ -333,6 +333,8 @@
         weights_row.append(links[k][2:3, :])
         source_row.append(from_line * n_aux + lane // links_per)
         keys_col.append(jnp.sum(jnp.where(diagonal, key, 0), axis=1, keepdims=True))
+    steps = [(st, c) for st in range(STAGES) for c in range(CHUNKS)]
+    hop_relay(*steps[0], 1)
     span = lines * lanes
     key = jnp.concatenate(keys_row, axis=1)
     column = jnp.concatenate(keys_col, axis=0)
@@ -350,6 +352,7 @@
     def picked(values):
         return jnp.sum(jnp.where(pick, values, 0), axis=1, keepdims=True)
 
+    hop_relay(*steps[1], 1)
     at = lax.broadcasted_iota(i32, (2 * half, 128), 1)
     table = jnp.where(at == 0, picked(jnp.concatenate(source_row, axis=1)), 0)
     table = jnp.where(at == 1, picked(jnp.concatenate(modes_row, axis=1)), table)
@@ -365,9 +368,7 @@
     lists[2 * half :] = jnp.broadcast_to(jnp.where(here > 0, upto, 0), (2 * n_aux, 128))
     planned = pltpu.make_async_copy(lists, plan, ins.at[2])
     planned.start()
-    steps = [(st, c) for st in range(STAGES) for c in range(CHUNKS)]
-    hop_relay(*steps[0], 1)
-    hop_relay(*steps[1], 1)
+    hop_relay(*steps[0], 2)
     planned.wait()
 
     mode_lane = lax.broadcasted_iota(i32, (rows_dev, mode_ref.shape[0]), 1)
@@ -406,7 +407,6 @@
         zero = jnp.zeros((rows, width), jnp.float32)
         lax.fori_loop(0, half, body, (zero, zero), unroll=12)
 
-    hop_relay(*steps[0], 2)
     for n, (st, c) in enumerate(steps):
         cut = slice(c * rows, (c + 1) * rows)
         both_cut = slice(c * pair, (c + 1) * pair)

time: 90.8 us -> 90.8 us (level)
  no operation moved by 1% of the time
where the time goes in v9:
time: 90.8 us; the launch traced here: 90.5 us
  Pallas kernels  86 us (95%)
  local copies, waits for them, and re-layouts  3.91 us (4%)
    pallas_call x1, Pallas kernels, by_states(): pl.pallas_call(functools.partial(kernel, lines, row_devs, half, count, pe...  86 us
    unnamed x4, local copies, waits for them, and re-layouts  2.42 us

profile of v9, /device:TPU:0, one launch (start us, length us, event | category | flops | bytes accessed | tf_op | source)
XLA Modules:
  0.0 90.5 jit_solution(17576718576267966143)
XLA Ops:
  0.6 0.8 copy.10
  1.4 0.1 reshape.7
  1.5 0.6 pad.4.link_ref
  2.1 86.0 %shard_map.86 = (f32[16,32,128]{2,1,0:T(8,128)}, f32[16,32,128]{2,1,0:T(8,128)}) custom-call(f32[16]{0:T(128)} %rate_ref.1, f32[2,128]{1,0:T(2,128)} %coef_ref.1, f32[16,32,128]{2,1,0:T(8,128)} %real_in.1, f32[16,32,128]{2,1,0:T(8,128)} %imag_in.1, f32[128,128]{1,0:T(8,128)} %ham_ref.1, f32[128,128]{1,0:T(8,128)} %mode_ref.1, s32[8,128]{1,0:T(8,128)} %pad.4.link_ref), custom_call_target="tpu_custom_call" | custom-call | tf_op jit(solution)/shard_map/pallas_call | solution.py:535
  88.1 0.0 copy-start
  88.1 1.7 %copy.13 = f32[16,32,128]{2,1,0:T(8,128)} copy(f32[16,32,128]{2,1,0:T(8,128)} %get-tuple-element.4) | data formatting | bytes 524288
  89.8 0.0 copy-done
  89.8 0.7 copy.14
Async XLA Ops:
  88.1 1.7 %copy-start = (f32[16,32,128]{2,1,0:T(8,128)S(1)}, f32[16,32,128]{2,1,0:T(8,128)}, u32[]{:S(2)}) copy-start(f32[16,32,128]{2,1,0:T(8,128)} %get-tuple-element.5) | copy-start | bytes 786436

commit v10 on v9

--- a/solution.py
+++ b/solution.py
@@ -412,6 +412,8 @@
         both_cut = slice(c * pair, (c + 1) * pair)
         for hop in range(3, lines):
             hop_relay(st, c, hop)
+        if n + 1 < len(steps):
+            hop_relay(*steps[n + 1], 2)
         gather_sum(st, c, 0)
 
         @pl.loop(0, n_aux, unroll=8)
@@ -419,8 +421,6 @@
             give[st][c][a] = run[plan[2 * half + a, 0]].astype(jnp.bfloat16)
 
         across = send(give[st][c], take[st][c], ys.at[st, c], yr.at[st, c], (beside, row))
-        if n + 1 < len(steps):
-            hop_relay(*steps[n + 1], 2)
         if n + 2 < len(steps):
             hop_relay(*steps[n + 2], 1)
         own = pl.ds(pl.multiple_of(line * n_aux, n_aux), n_aux)

time: 90.8 us -> 93.3 us (1.028)
  Pallas kernels: 86 us -> 88.5 us
    pallas_call x1, Pallas kernels: 86 us -> 88.5 us  [by_states(): pl.pallas_call(functools.partial(kernel, lines, row_devs, half, count, pe...]
where the time goes in v10:
time: 93.3 us; the launch traced here: 93.1 us
  Pallas kernels  88.5 us (95%)
  local copies, waits for them, and re-layouts  3.91 us (4%)
    pallas_call x1, Pallas kernels, by_states(): pl.pallas_call(functools.partial(kernel, lines, row_devs, half, count, pe...  88.5 us
    unnamed x4, local copies, waits for them, and re-layouts  2.42 us

profile of v10, /device:TPU:0, one launch (start us, length us, event | category | flops | bytes accessed | tf_op | source)
XLA Modules:
  0.0 93.1 jit_solution(13805252517719347187)
XLA Ops:
  0.6 0.8 copy.10
  1.4 0.1 reshape.7
  1.5 0.6 pad.4.link_ref
  2.1 88.5 %shard_map.86 = (f32[16,32,128]{2,1,0:T(8,128)}, f32[16,32,128]{2,1,0:T(8,128)}) custom-call(f32[16]{0:T(128)} %rate_ref.1, f32[2,128]{1,0:T(2,128)} %coef_ref.1, f32[16,32,128]{2,1,0:T(8,128)} %real_in.1, f32[16,32,128]{2,1,0:T(8,128)} %imag_in.1, f32[128,128]{1,0:T(8,128)} %ham_ref.1, f32[128,128]{1,0:T(8,128)} %mode_ref.1, s32[8,128]{1,0:T(8,128)} %pad.4.link_ref), custom_call_target="tpu_custom_call" | custom-call | tf_op jit(solution)/shard_map/pallas_call | solution.py:535
  90.6 0.0 copy-start
  90.6 1.7 %copy.13 = f32[16,32,128]{2,1,0:T(8,128)} copy(f32[16,32,128]{2,1,0:T(8,128)} %get-tuple-element.4) | data formatting | bytes 524288
  92.4 0.0 copy-done
  92.4 0.7 copy.14
Async XLA Ops:
  90.6 1.7 %copy-start = (f32[16,32,128]{2,1,0:T(8,128)S(1)}, f32[16,32,128]{2,1,0:T(8,128)}, u32[]{:S(2)}) copy-start(f32[16,32,128]{2,1,0:T(8,128)} %get-tuple-element.5) | copy-start | bytes 786436
